TPU v7x, 128 devices: a whole 4x4x4 slice. The times are simulated.
128 devices in a mesh: space: 64 (over z, y, x), mode: 2 (over core).
Axes of the slice: x: 4, y: 4, z: 4, core: 2. Of those that a mesh axis runs over, the one named last changes fastest.
Arguments:
- basis: float32 [256, 524288], P('mode', 'space'), as said below
- adjoint: float32 [256, 524288], P('mode', 'space'), as said below
- snapshots: float32 [32, 524288], P('mode', 'space'), as said below
- volumes: float32 [524288], P('space'), may hold values from 0.5 to 2, as said below
- singular: float32 [256], replicated, may hold values from 1 to 4
Outputs:
- new_basis: float32 [256, 524288], P('mode', 'space')
- new_singular: float32 [256], P('mode')
- hankel: float32 [256, 256], P('mode')
Inputs may be any that keep to these rules, and one draw needn't show every extreme that they name: `basis`: real values. `adjoint`: real values. `snapshots`: real values. Positive cell volumes.
All inputs are finite; a program needn't handle non-finite values.
Results may differ from a plain program's by a relative error of at most 0.00007.
Values sent between devices are 32-bit elements; how exact they have to be, the bound alone decides.
A program may use at most 128 MiB of HBM per device.

v0:
```python
import jax
import jax.numpy as jnp
from jax import lax
from jax.sharding import PartitionSpec as P

highest = lax.Precision.HIGHEST


def invert_lower(lower_factor):
    identity = jnp.eye(lower_factor.shape[0], dtype=lower_factor.dtype)
    return lax.linalg.triangular_solve(lower_factor, identity, left_side=True, lower=True)


def orthonormal(gram, row_block):
    lower_factor = jnp.linalg.cholesky(gram)
    return (lower_factor, jnp.dot(invert_lower(lower_factor), row_block, precision=highest))


def truncate(singular, project, triangle):
    full_width = singular.shape[0]
    snap_count = triangle.shape[0]
    upper_rows = jnp.concatenate([jnp.diag(singular), project], axis=1)
    lower_rows = jnp.concatenate(
        [jnp.zeros((snap_count, full_width), singular.dtype), triangle.T], axis=1
    )
    core_matrix = jnp.concatenate([upper_rows, lower_rows], axis=0)
    square = jnp.dot(core_matrix, core_matrix.T, precision=highest)
    leading = square[:, :full_width]
    lead_lower = jnp.linalg.cholesky(jnp.dot(leading.T, leading, precision=highest))
    rotate = jnp.dot(leading, invert_lower(lead_lower).T, precision=highest)
    energy = jnp.sum(rotate * jnp.dot(square, rotate, precision=highest), axis=0)
    return (rotate, jnp.sqrt(energy))


def shards(basis, adjoint, snapshots, volumes, singular):
    tile_rows, row_count = basis.shape
    mode_place = lax.axis_index("mode")
    scaled = volumes / float(row_count * lax.axis_size("space"))
    project_tile = jnp.dot(
        basis, (lax.all_gather(snapshots, "mode", axis=0, tiled=True) * scaled).T, precision=highest
    )
    project_tile = lax.psum(project_tile, "space")
    part_cols = project_tile
    removed = lax.psum_scatter(
        jnp.dot(part_cols.T, basis, precision=highest), "mode", scatter_dimension=0, tiled=True
    )
    residual, project = (
        lax.all_gather(snapshots - removed, "mode", axis=0, tiled=True),
        lax.all_gather(project_tile, "mode", axis=0, tiled=True),
    )
    adjoint_full = lax.all_gather(adjoint, "mode", axis=0, tiled=True)
    gram_one = lax.psum(jnp.dot(residual * scaled, residual.T, precision=highest), "space")
    triangle, ortho = orthonormal(gram_one, residual)
    rotate, new_singular = truncate(singular, project, triangle)
    full_width = singular.shape[0]
    own_columns = lax.dynamic_slice_in_dim(rotate, mode_place * tile_rows, tile_rows, 1)
    own_rows = lax.dynamic_slice_in_dim(rotate, mode_place * tile_rows, tile_rows, 0)
    part_cols = own_rows
    new_tile = lax.psum_scatter(
        jnp.dot(part_cols.T, basis, precision=highest), "mode", scatter_dimension=0, tiled=True
    )
    new_tile = new_tile + jnp.dot(own_columns[full_width:].T, ortho, precision=highest)
    hankel_rows = lax.psum(jnp.dot(new_tile * scaled, adjoint_full.T, precision=highest), "space")
    own_singular = lax.dynamic_slice_in_dim(new_singular, mode_place * tile_rows, tile_rows, 0)
    return (new_tile, own_singular, hankel_rows)


def solution(mesh):
    return jax.shard_map(
        shards,
        mesh=mesh,
        in_specs=(P("mode", "space"), P("mode", "space"), P("mode", "space"), P("space"), P()),
        out_specs=(P("mode", "space"), P("mode"), P("mode", None)),
        check_vma=False,
    )
```

profile of v0, /device:TPU:1, one launch (start us, length us, event | category | flops | bytes accessed | tf_op | source)
XLA Modules:
  0.0 1017.2 jit_solution(14659962462491865120)
XLA Ops:
  7.2 0.7 all-gather.4.cloned.1.call-update
  7.9 0.8 broadcast_multiply_fusion
  8.7 16.4 %all-gather.4.cloned.1.call-done = f32[32,8192]{1,0:T(8,128)} async-done(((f32[16,8192]{1,0:T(8,128)}), f32[32,8192]{1,0:T(8,128)}) %all-gather.4.cloned.1.call-update) | async-done | bytes 1048592 | tf_op jit(solution)/shard_map/all_gather | solution.py:40
  25.1 5.4 convolution_bitcast_fusion
  30.5 293.9 %psum.21 = f32[128,32]{1,0:T(8,128)S(1)} all-reduce(f32[128,32]{1,0:T(8,128)S(1)} %convolution_bitcast_fusion), channel_id=1, replica_groups=mesh['space'=64,'mode'=2] {'space'}, use_global_device_ids=true, to_apply=%region_0.0 | all-reduce | flops 4096 | bytes 32768 | tf_op jit(solution)/shard_map/psum | solution.py:42
  324.4 5.4 fusion.44
  329.9 59.7 %reduce-scatter.3.cloned.1.call-done = f32[16,8192]{1,0:T(8,128)} async-done(((f32[32,8192]{1,0:T(8,128)}), f32[16,8192]{1,0:T(8,128)}) %reduce-scatter.3.cloned.1.call-update) | async-done | bytes 524304 | tf_op jit(solution)/shard_map/reduce_scatter | solution.py:44
  389.6 1.9 sub.3
  391.6 0.1 broadcast_select_fusion
  391.7 1.9 all_gather.13
  393.6 11.4 %all-gather.6.cloned.1.call-done = f32[32,8192]{1,0:T(8,128)} async-done(((f32[16,8192]{1,0:T(8,128)}), f32[32,8192]{1,0:T(8,128)}) %all-gather.6.cloned.1.call-update) | async-done | bytes 1048592 | tf_op jit(solution)/shard_map/all_gather | solution.py:48
  405.0 2.6 fusion.3
  407.6 293.8 %psum.22 = f32[32,32]{0,1:T(8,128)S(1)} all-reduce(f32[32,32]{0,1:T(8,128)S(1)} %fusion.3), channel_id=1, replica_groups=mesh['space'=64,'mode'=2] {'space'}, use_global_device_ids=true, to_apply=%region_2.0 | all-reduce | flops 1024 | bytes 8192 | tf_op jit(solution)/shard_map/psum | solution.py:52
  701.4 2.9 cholesky.63
  704.4 0.6 compare_reduce_fusion.2
  705.0 0.7 select_bitcast_fusion.1
  705.8 1.0 fusion.9
  706.7 0.8 fusion.16
  707.6 0.1 copy.12
  707.8 11.7 %cholesky.128 = f32[128,128]{1,0:T(8,128)S(1)} custom-call(f32[128,128]{1,0:T(8,128)S(1)} %cholesky.157), custom_call_target="Cholesky" | custom-call | tf_op jit(solution)/shard_map/jit(cholesky)/cholesky | solution.py:29
  719.5 9.8 custom-call.20
  729.4 0.2 constant_dynamic-update-slice_fusion
  729.6 0.3 convolution_subtract_fusion.1
  729.8 11.9 %cholesky.145 = f32[128,128]{1,0:T(8,128)S(1)} custom-call(f32[128,128]{1,0:T(8,128)S(1)} %convolution_subtract_fusion.1), custom_call_target="Cholesky" | custom-call | tf_op jit(solution)/shard_map/jit(cholesky)/cholesky | solution.py:29
  741.7 0.6 compare_reduce_fusion
  743.8 4.0 while.1
  743.8 0.6 fusion.62
  744.4 1.4 bitcast_dynamic-update-slice_fusion.2
  745.8 0.6 fusion.62
  746.4 1.4 bitcast_dynamic-update-slice_fusion.2
  747.8 19.7 %custom-call.21 = f32[2,128,128]{1,2,0:T(8,128)S(1)} custom-call(f32[2,128,128]{2,1,0:T(8,128)S(1)} %get-tuple-element.10), custom_call_target="InvertDiagBlocksLowerTriangular" | custom-call | tf_op jit(solution)/shard_map/triangular_solve | solution.py:11
  767.5 0.3 fusion.26
  767.7 0.3 convolution_subtract_fusion
  768.0 0.3 fusion.29
  768.3 0.4 fusion.14
  768.8 10.6 %fusion.24 = f32[256,8192]{1,0:T(8,128)} fusion(f32[128,8192]{1,0:T(8,128)} %param.5, f32[288,256]{1,0:T(8,128)S(1)} %fusion.14, s32[]{:T(128)S(6)} %select_n.23), kind=kOutput, calls=%fused_computation.37 | convolution fusion | flops 3221225472 | bytes 12713988 | tf_op jit(solution)/shard_map/dot_general | solution.py:60
  779.4 0.5 all-gather.8.cloned.1.call-update
  780.0 2.4 custom-call.22
  782.5 0.2 fusion.34
  782.7 1.0 fusion.45
  783.7 63.6 %reduce-scatter.5.cloned.1.call-done = f32[128,8192]{1,0:T(8,128)} async-done(((f32[256,8192]{1,0:T(8,128)}), f32[128,8192]{1,0:T(8,128)}) %reduce-scatter.5.cloned.1.call-update) | async-done | bytes 4194320 | tf_op jit(solution)/shard_map/reduce_scatter | solution.py:59
  847.4 6.6 convolution_add_fusion
  854.0 18.9 %all-gather.8.cloned.1.call-done = f32[256,8192]{1,0:T(8,128)} async-done(((f32[128,8192]{1,0:T(8,128)}), f32[256,8192]{1,0:T(8,128)}) %all-gather.8.cloned.1.call-update) | async-done | bytes 8388624 | tf_op jit(solution)/shard_map/all_gather | solution.py:51
  872.9 13.6 %fusion = f32[128,256]{1,0:T(8,128)} fusion(f32[256,8192]{1,0:T(8,128)} %all-gather.8.cloned.1.call-done, f32[128,8192]{1,0:T(8,128)} %convolution_add_fusion, f32[8192]{0:T(1024)S(1)} %broadcast_multiply_fusion), kind=kOutput, calls=%fused_computation.3 | convolution fusion | flops 3222274048 | bytes 12746752 | tf_op jit(solution)/shard_map/dot_general | solution.py:63
  886.5 0.6 fusion.5
  887.2 0.6 dynamic_slice.11
  887.8 121.0 %all-reduce.4.cloned.1.call-done = f32[128,256]{1,0:T(8,128)} async-done(((f32[128,256]{1,0:T(8,128)}), f32[128,256]{1,0:T(8,128)}) %all-reduce.4.cloned.1.call-update) | async-done | bytes 131088 | tf_op jit(solution)/shard_map/psum | solution.py:63
  1008.7 1.6 copy.27
  (33 shorter events, 0.8 us)
Async XLA Ops:
  7.2 17.9 %all-gather.4.cloned.1.call-start = ((), (), s32[]{:S(2)}) async-start(), calls=%async_computation.2 | async-start | bytes 1572864 | tf_op jit(solution)/shard_map/all_gather | solution.py:40
  7.9 381.7 %reduce-scatter.3.cloned.1.call-start = ((), (), s32[]{:S(2)}) async-start(), calls=%async_computation.3 | async-start | bytes 1572864 | tf_op jit(solution)/shard_map/reduce_scatter | solution.py:44
  30.5 359.1 %copy-start.1 = (f32[16,8192]{1,0:T(8,128)S(1)}, f32[16,8192]{1,0:T(8,128)}, u32[]{:S(2)}) copy-start(f32[16,8192]{1,0:T(8,128)} %param.7) | copy-start | bytes 1572868
  324.4 67.2 %copy-start.2 = (f32[256]{0:T(256)S(1)}, f32[256]{0:T(256)}, u32[]{:S(2)}) copy-start(f32[256]{0:T(256)} %param.9) | copy-start | bytes 3076
  329.8 75.2 %all-gather.6.cloned.1.call-start = ((), (), s32[]{:S(2)}) async-start(), calls=%async_computation.4 | async-start | bytes 1572864 | tf_op jit(solution)/shard_map/all_gather | solution.py:48
  391.5 455.8 %reduce-scatter.5.cloned.1.call-start = ((), (), s32[]{:S(2)}) async-start(), calls=%async_computation.5 | async-start | bytes 12582912 | tf_op jit(solution)/shard_map/reduce_scatter | solution.py:59
  779.4 3.3 copy-start
  779.4 93.5 %all-gather.8.cloned.1.call-start = ((), (), s32[]{:S(2)}) async-start(), calls=%async_computation.6 | async-start | bytes 12582912 | tf_op jit(solution)/shard_map/all_gather | solution.py:51
  780.0 228.8 %all-reduce.4.cloned.1.call-start = ((), (), s32[]{:S(2)}) async-start(), calls=%async_computation.7 | async-start | bytes 262144 | tf_op jit(solution)/shard_map/psum | solution.py:63
Sparse Core Ops, SparseCore 0:
  9.7 15.3 all-gather.3
  330.0 59.5 reduce-scatter.2
  391.9 13.0 all-gather.5
  779.5 67.8 reduce-scatter.4
  848.9 24.0 all-gather.7
  886.7 122.0 all-reduce.3
where the time goes:
time: 1020 us
  blocking collectives  590 us (58%)
  waiting for transfers between devices  292 us (29%)
  other arithmetic  63.3 us (6%)
  matrix products  49.6 us (5%)
  between operations  15.6 us (2%)
    psum x1, blocking collectives, shards(): project_tile = lax.psum(project_tile, 'space')  294 us
    psum x1, blocking collectives, shards(): lax.psum(jnp.dot(residual * scaled, residual.T, precision=highest), 'space')  294 us
    reduce_scatter x2, waiting for transfers between devices, shards(): lax.psum_scatter(jnp.dot(part_cols.T, basis, precision=highest), 'mode',...  123 us
    psum x1, waiting for transfers between devices, shards(): lax.psum(jnp.dot(new_tile * scaled, adjoint_full.T, precision=highest), '...  121 us
    another operation x6, other arithmetic, truncate(): jnp.linalg.cholesky(jnp.dot(leading.T, leading, precision=highest))  34.1 us
    another operation x5, other arithmetic, invert_lower(): lax.linalg.triangular_solve(lower_factor, identity, left_side=True, lower...  22.8 us
  transfers between devices with their start and end apart: 6, of which 6 were waited for; matrix products, arithmetic and copies ran while one was open for 1% of the time, Pallas kernels for 0%

commit v1 on v0

v1 whole, which is shorter than its diff:
```python
import functools

import jax
import jax.numpy as jnp
from jax import lax
from jax.experimental import pallas as pl
from jax.experimental.pallas import tpu as pltpu
from jax.sharding import PartitionSpec as P

MESH = pl.DeviceIdType.MESH
highest = lax.Precision.HIGHEST
f32 = jnp.float32
bf16 = jnp.bfloat16
SIDE = 4
CHUNK = 1024


def split(value):
    high = value.astype(bf16)
    return high, (value - high.astype(f32)).astype(bf16)


def dot_nt(left, right):
    return lax.dot_general(left, right, (((1,), (1,)), ((), ())), preferred_element_type=f32)


def dot3(left, right):
    return dot_nt(left[0], right[0]) + (dot_nt(left[0], right[1]) + dot_nt(left[1], right[0]))


def exact_nt(left, right):
    return lax.dot_general(
        left, right, (((1,), (1,)), ((), ())), precision=highest, preferred_element_type=f32
    )


def exact_nn(left, right):
    return lax.dot_general(
        left, right, (((1,), (0,)), ((), ())), precision=highest, preferred_element_type=f32
    )


def gather_kernel(
    cells,
    basis, adjoint, snaps, volumes,
    other_out, snaps_out, project_out, gram_out, cross_out,
    own, other, adj, snap, root,
    own_hi, own_lo, adj_hi, adj_lo,
    acc_own, acc_other, cross,
    p_val, p_x, p_y, p_z, w_val, w_x, w_y, w_z, h_val, h_x, h_y, h_z, h_all,
    load_sem, adj_sem, small_sem, bs_sem, br_sem, ss_sem, out_sem,
    ps_sem, pr_sem, ws_sem, wr_sem, hs_sem, hr_sem,
):
    tile, width = own.shape
    snap_count = snap.shape[0]
    half = snap_count // 2
    chunks = width // CHUNK
    place = lax.axis_index("space")
    core = lax.axis_index("mode")
    peer_core = 1 - core
    x = lax.rem(place, SIDE)
    y = lax.rem(place // SIDE, SIDE)
    z = place // (SIDE * SIDE)

    def along(axis, step):
        if axis == "x":
            return place - x + lax.rem(x + step, SIDE)
        if axis == "y":
            return place + (lax.rem(y + step, SIDE) - y) * SIDE
        return place + (lax.rem(z + step, SIDE) - z) * (SIDE * SIDE)

    snap_rows = pl.ds(pl.multiple_of(core * half, half), half)
    load_snap = pltpu.make_async_copy(snaps, snap.at[snap_rows], small_sem.at[0])
    load_snap.start()

    def piece(k):
        return pl.ds(pl.multiple_of(k * CHUNK, CHUNK), CHUNK)

    def load_own(k):
        return pltpu.make_async_copy(basis.at[:, piece(k)], own.at[:, piece(k)], load_sem.at[k])

    def load_adj(k):
        return pltpu.make_async_copy(adjoint.at[:, piece(k)], adj.at[:, piece(k)], adj_sem.at[k])

    for k in range(chunks):
        load_own(k).start()
    for k in range(chunks):
        load_adj(k).start()

    barrier = pltpu.get_barrier_semaphore()
    friends = [(place, peer_core)]
    for step in range(1, SIDE):
        friends += [(along(axis, step), core) for axis in "xyz"]
        friends += [(along(axis, step), peer_core) for axis in "xz"]
    for friend in friends:
        pl.semaphore_signal(barrier, inc=1, device_id=friend, device_id_type=MESH)
    pl.semaphore_wait(barrier, len(friends))

    pair = (place, peer_core)

    def remote(src, dst, send_sem, recv_sem, device):
        return pltpu.make_async_remote_copy(
            src_ref=src, dst_ref=dst, send_sem=send_sem, recv_sem=recv_sem,
            device_id=device, device_id_type=MESH,
        )

    send_snap = remote(snaps, snap.at[snap_rows], ss_sem.at[0], ss_sem.at[1], pair)
    send_snap.start()

    def send_own(k):
        return remote(basis.at[:, piece(k)], other.at[:, piece(k)], bs_sem.at[k], br_sem.at[k], pair)

    for k in range(chunks):
        send_own(k).start()

    root[...] = jnp.sqrt(volumes[...] * (1.0 / cells))
    load_snap.wait()
    send_snap.wait()
    save_snap = pltpu.make_async_copy(snap, snaps_out, out_sem.at[0])
    save_snap.start()

    acc_own[...] = jnp.zeros_like(acc_own)
    acc_other[...] = jnp.zeros_like(acc_other)

    def first(k, carry):
        load_own(k).wait()
        cols = piece(k)
        rows = jnp.concatenate([own[:, cols], snap[:, cols]], axis=0) * root[:, cols]
        parts = split(rows)
        own_hi[:, cols], own_lo[:, cols] = parts
        acc_own[:, : tile + snap_count] += dot3(parts, parts)
        return carry

    lax.fori_loop(0, chunks, first, 0)

    def sends(src, buf, axis, send_sem, recv_sem, base, across):
        copies = []
        for step in range(1, SIDE):
            slot = base + step
            dst = buf.at[0, step] if across else buf.at[step]
            copies.append(
                remote(src, dst, send_sem.at[slot], recv_sem.at[slot], (along(axis, step), core))
            )
        if across:
            for step in range(SIDE):
                slot = base + SIDE + step
                copies.append(
                    remote(src, buf.at[1, step], send_sem.at[slot], recv_sem.at[slot],
                           (along(axis, step), peer_core))
                )
        for copy in copies:
            copy.start()
        return copies

    def waits(copies):
        for copy in copies:
            copy.wait()

    def four(value, buf):
        return (value + buf[2]) + (buf[1] + buf[3])

    p_val[0] = acc_own[tile : tile + snap_count, :tile]
    copies = sends(p_val.at[0], p_x, "x", ps_sem, pr_sem, 0, False)

    def second(k, carry):
        load_adj(k).wait()
        cols = piece(k)
        parts = split(adj[:, cols] * root[:, cols])
        adj_hi[:, cols], adj_lo[:, cols] = parts
        value = dot3((own_hi[:, cols], own_lo[:, cols]), parts)
        cross[:tile] += value[:tile]
        cross[2 * tile :] += value[tile:]
        return carry

    cross[...] = jnp.zeros_like(cross)
    lax.fori_loop(0, chunks, second, 0)

    waits(copies)
    p_val[1] = four(p_val[0], p_x)
    copies = sends(p_val.at[1], p_y, "y", ps_sem, pr_sem, SIDE, False)

    def third(k, carry):
        send_own(k).wait_recv()
        cols = piece(k)
        pltpu.make_async_copy(other.at[:, cols], other_out.at[:, cols], out_sem.at[k + 1]).start()
        left = split(other[:, cols] * root[:, cols])
        right = tuple(
            jnp.concatenate([a[:, cols], b[:tile, cols]], axis=0)
            for a, b in ((adj_hi, own_hi), (adj_lo, own_lo))
        )
        acc_other[...] += dot3(left, right)
        return carry

    lax.fori_loop(0, chunks // 2, third, 0)
    waits(copies)
    p_val[2] = four(p_val[1], p_y)
    copies = sends(p_val.at[2], p_z, "z", ps_sem, pr_sem, 2 * SIDE, True)
    lax.fori_loop(chunks // 2, chunks, third, 0)

    cross[tile : 2 * tile] = acc_other[:, :tile]
    quarter = cross.shape[0] // SIDE

    def quarter_rows(which):
        return pl.ds(pl.multiple_of(which * quarter, 8), quarter)

    h_copies = []
    for step in range(1, SIDE):
        h_copies.append(
            remote(cross.at[quarter_rows(lax.rem(x + step, SIDE))], h_x.at[step],
                   hs_sem.at[step], hr_sem.at[step], (along("x", step), core))
        )
        h_copies[-1].start()

    waits(copies)
    p_own = four(p_val[2], p_z.at[0])
    p_other = (p_z[1, 0] + p_z[1, 2]) + (p_z[1, 1] + p_z[1, 3])
    first_core = core == 0
    project_out[0] = jnp.where(first_core, p_own, p_other)
    project_out[1] = jnp.where(first_core, p_other, p_own)

    mixed = exact_nn(p_own, acc_own[:tile, :tile]) + exact_nn(p_other, acc_other[:, tile:])
    share = exact_nt(mixed, p_own) + 0.5 * acc_own[tile : tile + snap_count, tile : tile + snap_count]
    w_val[0] = jnp.concatenate([share, jnp.zeros((snap_count, tile - snap_count), f32)], axis=1)
    copies = sends(w_val.at[0], w_x, "x", ws_sem, wr_sem, 0, False)
    twice = 2.0 * (exact_nt(project_out[0], project_out[0]) + exact_nt(project_out[1], project_out[1]))

    waits(copies)
    w_val[1] = four(w_val[0], w_x)
    copies = sends(w_val.at[1], w_y, "y", ws_sem, wr_sem, SIDE, False)

    waits(h_copies)
    h_val[0] = four(cross[quarter_rows(x)], h_x)
    h_copies = sends(h_val.at[0], h_y, "y", hs_sem, hr_sem, SIDE, False)

    waits(copies)
    w_val[2] = four(w_val[1], w_y)
    copies = sends(w_val.at[2], w_z, "z", ws_sem, wr_sem, 2 * SIDE, True)

    waits(h_copies)
    h_val[1] = four(h_val[0], h_y)
    h_copies = sends(h_val.at[1], h_z, "z", hs_sem, hr_sem, 2 * SIDE, False)

    waits(copies)
    w_own = four(w_val[2], w_z.at[0])
    w_other = (w_z[1, 0] + w_z[1, 2]) + (w_z[1, 1] + w_z[1, 3])
    gram_out[...] = (w_own + w_other)[:, :snap_count] - twice

    waits(h_copies)
    h_val[2] = four(h_val[1], h_z)
    h_copies = []
    for side in range(2):
        for step in range(1 - side, SIDE):
            slot = 3 * SIDE + side * SIDE + step
            h_copies.append(
                remote(h_val.at[2], h_all.at[side, quarter_rows(x)],
                       hs_sem.at[slot], hr_sem.at[slot],
                       (along("x", step), core if side == 0 else peer_core))
            )
            h_copies[-1].start()
    h_index = 0
    for side in range(2):
        for step in range(1 - side, SIDE):
            slot = 3 * SIDE + side * SIDE + step
            h_copies[h_index].wait_send()
            h_index += 1
            sender = lax.rem(x + SIDE - step, SIDE)
            remote(h_val.at[2], h_all.at[side, quarter_rows(sender)],
                   hs_sem.at[slot], hr_sem.at[slot], pair).wait_recv()
    h_all[0, quarter_rows(x)] = h_val[2]
    cross_out[...] = h_all[...]

    def finish(k, carry):
        send_own(k).wait_send()
        pltpu.make_async_copy(other.at[:, piece(k)], other_out.at[:, piece(k)], out_sem.at[k + 1]).wait()
        return carry

    lax.fori_loop(0, chunks, finish, 0)
    save_snap.wait()


def gather(cells, basis, adjoint, snapshots, volumes):
    tile, width = basis.shape
    snap_count = 2 * snapshots.shape[0]
    rows = 2 * tile + snap_count
    quarter = rows // SIDE
    chunks = width // CHUNK
    dma = pltpu.SemaphoreType.DMA
    vmem = pltpu.VMEM
    any_spec = pl.BlockSpec(memory_space=pl.ANY)
    vmem_spec = pl.BlockSpec(memory_space=vmem)
    return pl.pallas_call(
        functools.partial(gather_kernel, cells),
        out_shape=(
            jax.ShapeDtypeStruct((tile, width), f32),
            jax.ShapeDtypeStruct((snap_count, width), f32),
            jax.ShapeDtypeStruct((2, snap_count, tile), f32),
            jax.ShapeDtypeStruct((snap_count, snap_count), f32),
            jax.ShapeDtypeStruct((2, rows, tile), f32),
        ),
        in_specs=[any_spec, any_spec, any_spec, vmem_spec],
        out_specs=(any_spec, any_spec, vmem_spec, vmem_spec, vmem_spec),
        scratch_shapes=[
            vmem((tile, width), f32),
            vmem((tile, width), f32),
            vmem((tile, width), f32),
            vmem((snap_count, width), f32),
            vmem((1, width), f32),
            vmem((tile + snap_count, width), bf16),
            vmem((tile + snap_count, width), bf16),
            vmem((tile, width), bf16),
            vmem((tile, width), bf16),
            vmem((tile + snap_count, 2 * tile), f32),
            vmem((tile, 2 * tile), f32),
            vmem((rows, tile), f32),
            vmem((3, snap_count, tile), f32),
            vmem((SIDE, snap_count, tile), f32),
            vmem((SIDE, snap_count, tile), f32),
            vmem((2, SIDE, snap_count, tile), f32),
            vmem((3, snap_count, tile), f32),
            vmem((SIDE, snap_count, tile), f32),
            vmem((SIDE, snap_count, tile), f32),
            vmem((2, SIDE, snap_count, tile), f32),
            vmem((3, quarter, tile), f32),
            vmem((SIDE, quarter, tile), f32),
            vmem((SIDE, quarter, tile), f32),
            vmem((SIDE, quarter, tile), f32),
            vmem((2, rows, tile), f32),
            dma((chunks,)),
            dma((chunks,)),
            dma((1,)),
            dma((chunks,)),
            dma((chunks,)),
            dma((2,)),
            dma((chunks + 1,)),
            dma((4 * SIDE,)),
            dma((4 * SIDE,)),
            dma((4 * SIDE,)),
            dma((4 * SIDE,)),
            dma((5 * SIDE,)),
            dma((5 * SIDE,)),
        ],
        compiler_params=pltpu.CompilerParams(
            collective_id=0, has_side_effects=True, vmem_limit_bytes=56 * 1024 * 1024
        ),
    )(basis, adjoint, snapshots, volumes)


def invert_lower(lower_factor):
    identity = jnp.eye(lower_factor.shape[0], dtype=lower_factor.dtype)
    return lax.linalg.triangular_solve(lower_factor, identity, left_side=True, lower=True)


def shards(basis, adjoint, snapshots, volumes, singular):
    tile, width = basis.shape
    core = lax.axis_index("mode")
    cells = float(width * lax.axis_size("space"))
    other, snaps, project_t, gram, cross = gather(
        cells, basis, adjoint, snapshots, volumes.reshape(1, width)
    )
    project = jnp.concatenate([project_t[0], project_t[1]], axis=1).T
    first_core = core == 0

    def ordered(mine, others):
        return jnp.where(first_core, mine, others), jnp.where(first_core, others, mine)

    swapped = jnp.concatenate([cross[1, tile : 2 * tile], cross[1, :tile], cross[1, 2 * tile :]], axis=0)
    left, right = ordered(cross[0], swapped)
    cross = jnp.concatenate([left, right], axis=1)
    top, bottom = ordered(cross[:tile], cross[tile : 2 * tile])
    squares = singular * singular
    core_top = jnp.diag(squares) + jnp.dot(project, project.T, precision=highest)
    core_side = jnp.dot(core_top, project, precision=highest) + jnp.dot(project, gram, precision=highest)
    gram_lead = core_top * squares + jnp.dot(core_side, project.T, precision=highest)
    gram_lead = 0.5 * (gram_lead + gram_lead.T)
    inverse = invert_lower(jnp.linalg.cholesky(gram_lead))
    inverse = lax.dynamic_slice_in_dim(inverse, core * tile, tile, 0)
    energy = jnp.sum(jnp.square(jnp.dot(inverse, core_top * singular, precision=highest)), axis=1)
    energy = energy + jnp.sum(jnp.square(jnp.dot(inverse, core_side, precision=highest)), axis=1)
    on_modes = inverse * squares
    on_snaps = jnp.dot(inverse, project, precision=highest)
    hankel = (
        jnp.dot(on_modes[:, :tile], top, precision=highest)
        + jnp.dot(on_modes[:, tile:], bottom, precision=highest)
        + jnp.dot(on_snaps, cross[2 * tile :], precision=highest)
    )
    on_first, on_second = on_modes[:, :tile], on_modes[:, tile:]
    on_own, on_other = ordered(on_first, on_second)
    new_tile = (
        jnp.dot(on_own, basis, precision=highest)
        + jnp.dot(on_other, other, precision=highest)
        + jnp.dot(on_snaps, snaps, precision=highest)
    )
    return new_tile, jnp.sqrt(energy), hankel


def solution(mesh):
    return jax.shard_map(
        shards,
        mesh=mesh,
        in_specs=(P("mode", "space"), P("mode", "space"), P("mode", "space"), P("space"), P()),
        out_specs=(P("mode", "space"), P("mode"), P("mode", None)),
        check_vma=False,
    )
```

time: 1020 us -> 130 us (0.13)
  blocking collectives: 590 us -> 0 us
  waiting for transfers between devices: 292 us -> 0 us
  Pallas kernels: 0 us -> 44.2 us
  matrix products: 49.6 us -> 20.2 us
  between operations: 15.6 us -> 2.18 us
    psum x2 -> x0, blocking collectives: 588 us -> none  [the longest x1 294 us: shards(): project_tile = lax.psum(project_tile, 'space')]
    reduce_scatter x2 -> x0, waiting for transfers between devices: 123 us -> none  [shards(): lax.psum_scatter(jnp.dot(part_cols.T, basis, precision=highest), 'mode',...]
    psum x1 -> x0, waiting for transfers between devices: 121 us -> none  [shards(): lax.psum(jnp.dot(new_tile * scaled, adjoint_full.T, precision=highest), '...]
    all_gather x3 -> x0, waiting for transfers between devices: 46.7 us -> none  [the longest x1 18.9 us: shards(): adjoint_full = lax.all_gather(adjoint, 'mode', axis=0, tiled=True)]
    pallas_call x0 -> x1, Pallas kernels: none -> 44.2 us  [gather(): pl.pallas_call(functools.partial(gather_kernel, cells), out_shape=(jax.Sh...]
    dot_general x11 -> x13, matrix products: 48 us -> 18.9 us  [the longest x1 5.55 us: shards(): jnp.dot(on_own, basis, precision=highest)]
    another operation x9 -> x7, other arithmetic: 37.7 us -> 34.6 us  [shards(): inverse = invert_lower(jnp.linalg.cholesky(gram_lead))]
    another operation x5 -> x3, other arithmetic: 22.8 us -> 19.9 us  [invert_lower(): lax.linalg.triangular_solve(lower_factor, identity, left_side=True, lower...]
  transfers between devices with their start and end apart: 6 -> 0, of which waited for: 6 -> 0; matrix products, arithmetic and copies ran while one was open for 1% -> 0% of each run, Pallas kernels for 0% -> 0%
where the time goes in v1:
time: 130 us
  other arithmetic  56.9 us (44%)
  Pallas kernels  44.2 us (34%)
  matrix products  20.2 us (16%)
  local copies, waits for them, and re-layouts  5.97 us (5%)
  between operations  2.18 us (2%)
    pallas_call x1, Pallas kernels, gather(): pl.pallas_call(functools.partial(gather_kernel, cells), out_shape=(jax.Sh...  44.2 us
    another operation x7, other arithmetic, shards(): inverse = invert_lower(jnp.linalg.cholesky(gram_lead))  34.6 us
    another operation x3, other arithmetic, invert_lower(): lax.linalg.triangular_solve(lower_factor, identity, left_side=True, lower...  19.9 us
    dot_general x1, matrix products, shards(): jnp.dot(on_own, basis, precision=highest)  5.55 us
    dot_general x1, matrix products, shards(): jnp.dot(on_snaps, snaps, precision=highest)  5.02 us
    another operation x6, local copies, waits for them, and re-layouts  3.95 us
    dot_general x1, matrix products, shards(): jnp.dot(on_other, other, precision=highest)  3.72 us

profile of v1, /device:TPU:1, one launch (start us, length us, event | category | flops | bytes accessed | tf_op | source)
XLA Modules:
  0.0 129.6 jit_solution(5091940959340714541)
XLA Ops:
  0.6 0.1 triangular_solve.69
  0.7 0.8 mul.40
  1.5 44.2 %shard_map.76 = (f32[128,8192]{1,0:T(8,128)}, f32[32,8192]{1,0:T(8,128)}, f32[2,32,128]{2,1,0:T(8,128)}, f32[32,32]{1,0:T(8,128)}, f32[2,288,128]{2,1,0:T(8,128)}) custom-call(f32[128,8192]{1,0:T(8,128)} %basis.1, f32[128,8192]{1,0:T(8,128)} %adjoint.1, f32[16,8192]{1,0:T(8,128)} %snaps.1, f32[1,8192]{1,0:T(1,128)} %bitcast.66), custom_call_target="tpu_custom_call" | custom-call | tf_op jit(solution)/shard_map/pallas_call | solution.py:291
  45.8 0.8 slice_bitcast_fusion.8
  46.5 0.0 copy-start.2
  46.5 0.9 slice_bitcast_fusion.5
  47.4 0.9 bitcast_select_fusion.1
  48.4 0.4 fusion.44
  48.8 0.4 fusion.8
  49.2 0.9 convolution_add_fusion.3
  50.2 0.4 fusion.43
  50.6 0.1 copy.9
  50.7 0.1 copy.8
  50.9 0.1 fusion.5
  51.0 11.7 %cholesky.49 = f32[128,128]{1,0:T(8,128)S(1)} custom-call(f32[128,128]{1,0:T(8,128)S(1)} %cholesky.115), custom_call_target="Cholesky" | custom-call | tf_op jit(solution)/shard_map/jit(cholesky)/cholesky | solution.py:375
  62.8 0.6 compare_reduce_fusion.1
  63.4 9.8 %custom-call.14 = f32[1,128,128]{1,2,0:T(8,128)S(1)} custom-call(f32[1,128,128]{2,1,0:T(8,128)S(1)} %get-tuple-element.40), custom_call_target="InvertDiagBlocksLowerTriangular" | custom-call | tf_op jit(solution)/shard_map/jit(cholesky)/cholesky | solution.py:375
  73.3 0.2 constant_dynamic-update-slice_fusion
  73.5 0.3 convolution_subtract_fusion.1
  73.7 11.7 %cholesky.103 = f32[128,128]{1,0:T(8,128)S(1)} custom-call(f32[128,128]{1,0:T(8,128)S(1)} %convolution_subtract_fusion.1), custom_call_target="Cholesky" | custom-call | tf_op jit(solution)/shard_map/jit(cholesky)/cholesky | solution.py:375
  85.5 0.6 compare_reduce_fusion
  87.5 4.0 %while.1 = (s32[]{:T(128)}, f32[256,256]{1,0:T(8,128)S(1)}, s32[2,2]{1,0:T(2,128)S(1)}, f32[2,128,128]{2,1,0:T(8,128)S(1)}, s32[]{:T(128)}) while((s32[]{:T(128)}, f32[256,256]{1,0:T(8,128)S(1)}, s32[2,2]{1,0:T(2,128)S(1)}, f32[2,128,128]{2,1,0:T(8,128)S(1)}, s32[]{:T(128)}) %tuple.31), condition=%wide.while_cond, body=%wide.while_body.sunk | while | flops 2 | bytes 131189 | solution.py:350
  87.5 0.6 fusion.77
  88.1 1.4 %bitcast_dynamic-update-slice_fusion.2 = f32[2,128,128]{2,1,0:T(8,128)S(1)} fusion(f32[2,128,128]{2,1,0:T(8,128)S(1)} %get-tuple-element.83, s32[]{:T(128)S(6)} %copy.15, f32[256,256]{1,0:T(8,128)S(1)} %get-tuple-element.86, s32[]{:T(128)} %bitcast.64, s32[]{:T(128)} %bitcast.65), kind=kLoop, calls=%fused_computation.clone.1 | loop fusion | bytes 131084 | tf_op jit(solution)/shard_map/triangular_solve
  89.5 0.6 fusion.77
  90.1 1.4 %bitcast_dynamic-update-slice_fusion.2 = f32[2,128,128]{2,1,0:T(8,128)S(1)} fusion(f32[2,128,128]{2,1,0:T(8,128)S(1)} %get-tuple-element.83, s32[]{:T(128)S(6)} %copy.15, f32[256,256]{1,0:T(8,128)S(1)} %get-tuple-element.86, s32[]{:T(128)} %bitcast.64, s32[]{:T(128)} %bitcast.65), kind=kLoop, calls=%fused_computation.clone.1 | loop fusion | bytes 131084 | tf_op jit(solution)/shard_map/triangular_solve
  91.5 19.9 %custom-call.15 = f32[2,128,128]{1,2,0:T(8,128)S(1)} custom-call(f32[2,128,128]{2,1,0:T(8,128)S(1)} %get-tuple-element.20), custom_call_target="InvertDiagBlocksLowerTriangular" | custom-call | tf_op jit(solution)/shard_map/triangular_solve | solution.py:350
  111.3 0.3 fusion.20
  111.6 0.3 convolution_subtract_fusion
  111.9 0.3 fusion.23
  112.2 0.1 broadcast_multiply_fusion
  112.3 0.0 copy-done.2
  112.3 0.4 fusion.1
  112.7 0.3 fusion.2
  113.0 0.2 fusion.42
  113.2 0.5 add_sqrt_fusion
  113.7 0.3 fusion.38
  114.1 0.3 fusion.13
  114.3 0.9 fusion
  115.3 0.0 copy-start
  115.3 5.6 %fusion.28 = f32[128,8192]{1,0:T(8,128)S(1)} fusion(f32[128,8192]{1,0:T(8,128)} %basis.1, f32[128,256]{1,0:T(8,128)S(1)} %get-tuple-element.29, pred[]{:T(512)S(6)} %eq.17), kind=kOutput, calls=%fused_computation.58 | convolution fusion | flops 1610629120 | bytes 8519681 | tf_op jit(solution)/shard_map/dot_general | solution.py:389
  120.8 0.0 copy-done
  120.8 0.0 copy-start.1
  120.8 3.7 %convolution_add_fusion.1 = f32[128,8192]{1,0:T(8,128)S(1)} fusion(f32[128,8192]{1,0:T(8,128)S(1)} %fusion.28, f32[128,8192]{1,0:T(8,128)S(1)} %copy-done, f32[128,256]{1,0:T(8,128)S(1)} %get-tuple-element.29, pred[]{:T(512)S(6)} %eq.17), kind=kOutput, calls=%fused_computation.3 | convolution fusion | flops 1611677696 | bytes 12713985 | tf_op jit(solution)/shard_map/dot_general | solution.py:390
  124.6 0.0 copy-done.1
  124.6 5.0 %convolution_add_fusion = f32[128,8192]{1,0:T(8,128)} fusion(f32[128,8192]{1,0:T(8,128)S(1)} %convolution_add_fusion.1, f32[128,32]{0,1:T(8,128)S(1)} %fusion.42, f32[32,8192]{1,0:T(8,128)S(1)} %copy-done.1), kind=kOutput, calls=%fused_computation.2 | convolution fusion | flops 403701760 | bytes 9453568 | tf_op jit(solution)/shard_map/dot_general | solution.py:391
  (10 shorter events, 0.2 us)
Async XLA Ops:
  46.5 65.7 %copy-start.2 = (f32[256]{0:T(256)S(1)}, f32[256]{0:T(256)}, u32[]{:S(2)}) copy-start(f32[256]{0:T(256)} %param.9) | copy-start | bytes 3076
  115.3 5.6 %copy-start = (f32[128,8192]{1,0:T(8,128)S(1)}, f32[128,8192]{1,0:T(8,128)}, u32[]{:S(2)}) copy-start(f32[128,8192]{1,0:T(8,128)} %get-tuple-element.10) | copy-start | bytes 12582916
  120.8 3.7 %copy-start.1 = (f32[32,8192]{1,0:T(8,128)S(1)}, f32[32,8192]{1,0:T(8,128)}, u32[]{:S(2)}) copy-start(f32[32,8192]{1,0:T(8,128)} %get-tuple-element.11) | copy-start | bytes 3145732

commit v2 on v1

--- a/solution.py
+++ b/solution.py
@@ -345,52 +345,191 @@
     )(basis, adjoint, snapshots, volumes)
 
 
-def invert_lower(lower_factor):
-    identity = jnp.eye(lower_factor.shape[0], dtype=lower_factor.dtype)
-    return lax.linalg.triangular_solve(lower_factor, identity, left_side=True, lower=True)
+def dot_nn(left, right):
+    return lax.dot_general(left, right, (((1,), (0,)), ((), ())), preferred_element_type=f32)
+
+
+def dot3_nn(left, right):
+    rows = left[0].shape[0]
+    both = dot_nn(jnp.concatenate([left[0], left[1]], axis=0), right[0])
+    return both[:rows] + (dot_nn(left[0], right[1]) + both[rows:])
+
+
+def exact_tn(left, right):
+    return lax.dot_general(
+        left, right, (((0,), (0,)), ((), ())), precision=highest, preferred_element_type=f32
+    )
+
+
+def inverse_factor(block, group):
+    size = block.shape[0]
+    eye = (
+        lax.broadcasted_iota(jnp.int32, (size, size), 0)
+        == lax.broadcasted_iota(jnp.int32, (size, size), 1)
+    ).astype(f32)
+    left = jnp.concatenate([block, eye], axis=1)
+    done = []
+    for start in range(0, size, group):
+        count = size - start
+        row = lax.broadcasted_iota(jnp.int32, (count, 2 * size), 0)
+        cols = [
+            jnp.broadcast_to(left[:, start + t : start + t + 1], (count, 2 * size))
+            for t in range(group)
+        ]
+        for t in range(group):
+            pivot = cols[t][t : t + 1, :]
+            factor = jnp.where(row > t, cols[t], 0.0) * (1.0 / pivot)
+            for u in range(t + 1, group):
+                cols[u] = cols[u] - factor * cols[u][t : t + 1, :]
+            done.append(left[t : t + 1, :] * lax.rsqrt(pivot))
+            left = left - factor * left[t : t + 1, :]
+        left = left[group:]
+    return jnp.concatenate(done, axis=0)[:, size:]
+
+
+def rotate_kernel(
+    basis, other, snaps, project, gram, cross, singular,
+    new_out, singular_out, hankel_out,
+    rows, result, lead, inverse, coef_hi, coef_lo, in_sem, out_sem,
+):
+    tile, width = result.shape
+    modes = 2 * tile
+    snap_count = snaps.shape[0]
+    chunks = width // CHUNK
+    core = lax.axis_index("mode")
+    first_core = core == 0
+
+    def piece(k):
+        return pl.ds(pl.multiple_of(k * CHUNK, CHUNK), CHUNK)
+
+    def loads(k):
+        cols = piece(k)
+        return (
+            pltpu.make_async_copy(basis.at[:, cols], rows.at[:tile, cols], in_sem.at[0, k]),
+            pltpu.make_async_copy(other.at[:, cols], rows.at[tile:modes, cols], in_sem.at[1, k]),
+            pltpu.make_async_copy(snaps.at[:, cols], rows.at[modes:, cols], in_sem.at[2, k]),
+        )
+
+    for k in range(chunks):
+        for copy in loads(k):
+            copy.start()
+
+    s = singular[...]
+    s2 = s * s
+    project_t = jnp.concatenate([project[0], project[1]], axis=1)
+    scaled_t = project_t * s2
+    pad = jnp.zeros((tile - 2 * snap_count, modes), f32)
+    turned = jnp.concatenate([project_t, scaled_t, pad], axis=0).T
+    by_mode, by_mode_scaled = turned[:, :snap_count], turned[:, snap_count : 2 * snap_count]
+    inner = exact_nt(project_t, project_t) + gram[...]
+    side = by_mode_scaled + exact_nn(by_mode, inner)
+    side_and_project = jnp.concatenate([side, by_mode], axis=1)
+    eye = lax.broadcasted_iota(jnp.int32, (modes, modes), 0) == lax.broadcasted_iota(
+        jnp.int32, (modes, modes), 1
+    )
+    lead[...] = jnp.where(eye, s2 * s2, 0.0) + exact_nt(
+        side_and_project, turned[:, : 2 * snap_count]
+    )
+    inverse[...] = eye.astype(f32)
+    size = 64
+    for start in range(0, modes, size):
+        stop = start + size
+        small = inverse_factor(lead[start:stop, start:stop], 8)
+        part = exact_nn(small, inverse[start:stop, :])
+        inverse[start:stop, :] = part
+        if stop < modes:
+            upper = exact_nn(small, lead[start:stop, :])
+            later = upper[:, stop:]
+            lead[stop:, :] -= exact_tn(later, upper)
+            inverse[stop:, :] -= exact_tn(later, part)
+
+    mine = inverse[pl.ds(pl.multiple_of(core * tile, tile), tile), :]
+    both = exact_nn(mine, side_and_project)
+    on_snaps = both[:, snap_count:]
+    on_modes = mine * s2
+    image = (on_modes + exact_nn(on_snaps, project_t)) * s
+    energy = exact_nt(jnp.ones((8, modes), f32), image * image) + exact_nt(
+        jnp.ones((8, snap_count), f32), both[:, :snap_count] * both[:, :snap_count]
+    )
+    singular_out[...] = jnp.sqrt(energy[:1])
+
+    on_first, on_second = on_modes[:, :tile], on_modes[:, tile:]
+    coef = split(
+        jnp.concatenate(
+            [
+                jnp.where(first_core, on_first, on_second),
+                jnp.where(first_core, on_second, on_first),
+                on_snaps,
+            ],
+            axis=1,
+        )
+    )
+    coef_hi[...], coef_lo[...] = coef
+
+    def rotate(k, carry):
+        for copy in loads(k):
+            copy.wait()
+        cols = piece(k)
+        result[:, cols] = dot3_nn((coef_hi[...], coef_lo[...]), split(rows[:, cols]))
+        pltpu.make_async_copy(result.at[:, cols], new_out.at[:, cols], out_sem.at[k]).start()
+        return carry
+
+    lax.fori_loop(0, chunks, rotate, 0)
+
+    swapped = jnp.concatenate([cross[1, tile:modes], cross[1, :tile], cross[1, modes:]], axis=0)
+    columns = jnp.concatenate(
+        [jnp.where(first_core, cross[0], swapped), jnp.where(first_core, swapped, cross[0])], axis=1
+    )
+    hankel_out[...] = dot3_nn(coef, split(columns))
+
+    def finish(k, carry):
+        pltpu.make_async_copy(result.at[:, piece(k)], new_out.at[:, piece(k)], out_sem.at[k]).wait()
+        return carry
+
+    lax.fori_loop(0, chunks, finish, 0)
+
+
+def rotate(basis, other, snaps, project, gram, cross, singular):
+    tile, width = basis.shape
+    modes, snap_count = 2 * tile, snaps.shape[0]
+    chunks = width // CHUNK
+    dma = pltpu.SemaphoreType.DMA
+    vmem = pltpu.VMEM
+    any_spec = pl.BlockSpec(memory_space=pl.ANY)
+    vmem_spec = pl.BlockSpec(memory_space=vmem)
+    return pl.pallas_call(
+        rotate_kernel,
+        out_shape=(
+            jax.ShapeDtypeStruct((tile, width), f32),
+            jax.ShapeDtypeStruct((1, tile), f32),
+            jax.ShapeDtypeStruct((tile, modes), f32),
+        ),
+        in_specs=[any_spec] * 3 + [vmem_spec] * 4,
+        out_specs=(any_spec, vmem_spec, vmem_spec),
+        scratch_shapes=[
+            vmem((modes + snap_count, width), f32),
+            vmem((tile, width), f32),
+            vmem((modes, modes), f32),
+            vmem((modes, modes), f32),
+            vmem((tile, modes + snap_count), bf16),
+            vmem((tile, modes + snap_count), bf16),
+            dma((3, chunks)),
+            dma((chunks,)),
+        ],
+        compiler_params=pltpu.CompilerParams(vmem_limit_bytes=56 * 1024 * 1024),
+    )(basis, other, snaps, project, gram, cross, singular)
 
 
 def shards(basis, adjoint, snapshots, volumes, singular):
     tile, width = basis.shape
-    core = lax.axis_index("mode")
     cells = float(width * lax.axis_size("space"))
-    other, snaps, project_t, gram, cross = gather(
+    other, snaps, project, gram, cross = gather(
         cells, basis, adjoint, snapshots, volumes.reshape(1, width)
     )
-    project = jnp.concatenate([project_t[0], project_t[1]], axis=1).T
-    first_core = core == 0
-
-    def ordered(mine, others):
-        return jnp.where(first_core, mine, others), jnp.where(first_core, others, mine)
-
-    swapped = jnp.concatenate([cross[1, tile : 2 * tile], cross[1, :tile], cross[1, 2 * tile :]], axis=0)
-    left, right = ordered(cross[0], swapped)
-    cross = jnp.concatenate([left, right], axis=1)
-    top, bottom = ordered(cross[:tile], cross[tile : 2 * tile])
-    squares = singular * singular
-    core_top = jnp.diag(squares) + jnp.dot(project, project.T, precision=highest)
-    core_side = jnp.dot(core_top, project, precision=highest) + jnp.dot(project, gram, precision=highest)
-    gram_lead = core_top * squares + jnp.dot(core_side, project.T, precision=highest)
-    gram_lead = 0.5 * (gram_lead + gram_lead.T)
-    inverse = invert_lower(jnp.linalg.cholesky(gram_lead))
-    inverse = lax.dynamic_slice_in_dim(inverse, core * tile, tile, 0)
-    energy = jnp.sum(jnp.square(jnp.dot(inverse, core_top * singular, precision=highest)), axis=1)
-    energy = energy + jnp.sum(jnp.square(jnp.dot(inverse, core_side, precision=highest)), axis=1)
-    on_modes = inverse * squares
-    on_snaps = jnp.dot(inverse, project, precision=highest)
-    hankel = (
-        jnp.dot(on_modes[:, :tile], top, precision=highest)
-        + jnp.dot(on_modes[:, tile:], bottom, precision=highest)
-        + jnp.dot(on_snaps, cross[2 * tile :], precision=highest)
-    )
-    on_first, on_second = on_modes[:, :tile], on_modes[:, tile:]
-    on_own, on_other = ordered(on_first, on_second)
-    new_tile = (
-        jnp.dot(on_own, basis, precision=highest)
-        + jnp.dot(on_other, other, precision=highest)
-        + jnp.dot(on_snaps, snaps, precision=highest)
-    )
-    return new_tile, jnp.sqrt(energy), hankel
+    new_tile, new_singular, hankel = rotate(
+        basis, other, snaps, project, gram, cross, singular.reshape(1, 2 * tile)
+    )
+    return new_tile, new_singular.reshape(tile), hankel
 
 
 def solution(mesh):

time: 130 us -> 63.7 us (0.49)
  other arithmetic: 56.9 us -> 0 us
  matrix products: 20.2 us -> 0 us
  Pallas kernels: 44.2 us -> 62.9 us
  local copies, waits for them, and re-layouts: 5.97 us -> 0 us
  between operations: 2.18 us -> 0.64 us
    another operation x10 -> x0, other arithmetic: 54.5 us -> none  [the longest x7 34.6 us: shards(): inverse = invert_lower(jnp.linalg.cholesky(gram_lead))]
    dot_general x13 -> x0, matrix products: 18.9 us -> none  [the longest x1 5.55 us: shards(): jnp.dot(on_own, basis, precision=highest)]
    pallas_call x0 -> x1, Pallas kernels: none -> 18.6 us  [rotate(): pl.pallas_call(rotate_kernel, out_shape=(jax.ShapeDtypeStruct((tile, widt...]
    another operation x9 -> x0, local copies, waits for them, and re-layouts: 4.05 us -> none
    squeeze x2 -> x0, local copies, waits for them, and re-layouts: 1.65 us -> none  [the longest x1 0.89 us: shards(): cross[1, tile:2 * tile]]
    another operation x5 -> x0, matrix products: 1.3 us -> none  [the longest x3 0.83 us: invert_lower(): lax.linalg.triangular_solve(lower_factor, identity, left_side=True, lower...]
where the time goes in v2:
time: 63.7 us; the launch traced here: 63.5 us
  Pallas kernels  62.9 us (99%)
  between operations  0.64 us (1%)
    pallas_call x1, Pallas kernels, gather(): pl.pallas_call(functools.partial(gather_kernel, cells), out_shape=(jax.Sh...  44.2 us
    pallas_call x1, Pallas kernels, rotate(): pl.pallas_call(rotate_kernel, out_shape=(jax.ShapeDtypeStruct((tile, widt...  18.6 us

profile of v2, /device:TPU:1, one launch (start us, length us, event | category | flops | bytes accessed | tf_op | source)
XLA Modules:
  0.0 63.5 jit_solution(4924054005047941425)
XLA Ops:
  0.6 44.2 %shard_map.76 = (f32[128,8192]{1,0:T(8,128)}, f32[32,8192]{1,0:T(8,128)}, f32[2,32,128]{2,1,0:T(8,128)}, f32[32,32]{1,0:T(8,128)}, f32[2,288,128]{2,1,0:T(8,128)}) custom-call(f32[128,8192]{1,0:T(8,128)} %basis.3, f32[128,8192]{1,0:T(8,128)} %adjoint.1, f32[16,8192]{1,0:T(8,128)} %snaps.1, f32[1,8192]{1,0:T(1,128)} %bitcast.3), custom_call_target="tpu_custom_call" | custom-call | tf_op jit(solution)/shard_map/pallas_call | solution.py:291
  44.9 18.6 %shard_map.77 = (f32[128,8192]{1,0:T(8,128)}, f32[1,128]{1,0:T(1,128)}, f32[128,256]{1,0:T(8,128)}) custom-call(f32[128,8192]{1,0:T(8,128)} %basis.3, f32[128,8192]{1,0:T(8,128)} %get-tuple-element.11.other, f32[32,8192]{1,0:T(8,128)} %get-tuple-element.12.snaps, f32[2,32,128]{2,1,0:T(8,128)} %get-tuple-element.13.project, f32[32,32]{1,0:T(8,128)} %get-tuple-element.14.gram, ...), custom_call_target="tpu_custom_call" | custom-call | tf_op jit(solution)/shard_map/pallas_call | solution.py:500

commit v3 on v2

v3 whole, which is shorter than its diff:
```python
import functools

import jax
import jax.numpy as jnp
from jax import lax
from jax.experimental import pallas as pl
from jax.experimental.pallas import tpu as pltpu
from jax.sharding import PartitionSpec as P

MESH = pl.DeviceIdType.MESH
highest = lax.Precision.HIGHEST
f32 = jnp.float32
bf16 = jnp.bfloat16
SIDE = 4
PLANE = SIDE * SIDE
CHUNK = 1024


def split(value):
    high = value.astype(bf16)
    return high, (value - high.astype(f32)).astype(bf16)


def dot_nt(left, right):
    return lax.dot_general(left, right, (((1,), (1,)), ((), ())), preferred_element_type=f32)


def dot3(left, right):
    return dot_nt(left[0], right[0]) + (dot_nt(left[0], right[1]) + dot_nt(left[1], right[0]))


def exact_nt(left, right):
    return lax.dot_general(
        left, right, (((1,), (1,)), ((), ())), precision=highest, preferred_element_type=f32
    )


def exact_nn(left, right):
    return lax.dot_general(
        left, right, (((1,), (0,)), ((), ())), precision=highest, preferred_element_type=f32
    )


def gather_kernel(
    cells,
    basis, adjoint, snaps, volumes,
    other_out, snaps_out, total_out,
    own, other, adj, snap, root,
    left_hi, left_lo, adj_hi, adj_lo,
    acc, acc_snap, share, slots, part, z_slots, total,
    load_sem, adj_sem, small_sem, bs_sem, br_sem, ss_sem, out_sem,
    rs_sem, rr_sem, zs_sem, zr_sem, gs_sem, gr_sem, fs_sem, fr_sem,
):
    tile, width = own.shape
    snap_count = snap.shape[0]
    half = snap_count // 2
    chunks = width // CHUNK
    near = tile + snap_count
    place = lax.axis_index("space")
    core = lax.axis_index("mode")
    pair = (place, 1 - core)
    spot = lax.rem(place, PLANE)
    level = place // PLANE

    def in_plane(step):
        return lax.rem(spot + step, PLANE)

    def plane_peer(step):
        return (level * PLANE + in_plane(step), core)

    def level_peer(step):
        return (lax.rem(level + step, SIDE) * PLANE + spot, core)

    def piece(k):
        return pl.ds(pl.multiple_of(k * CHUNK, CHUNK), CHUNK)

    def load_own(k):
        return pltpu.make_async_copy(basis.at[:, piece(k)], own.at[:, piece(k)], load_sem.at[k])

    def load_adj(k):
        return pltpu.make_async_copy(adjoint.at[:, piece(k)], adj.at[:, piece(k)], adj_sem.at[k])

    def remote(src, dst, send_sem, recv_sem, device):
        return pltpu.make_async_remote_copy(
            src_ref=src, dst_ref=dst, send_sem=send_sem, recv_sem=recv_sem,
            device_id=device, device_id_type=MESH,
        )

    barrier = pltpu.get_barrier_semaphore()
    friends = [pair]
    friends += [plane_peer(step) for step in range(1, PLANE)]
    friends += [level_peer(step) for step in range(1, SIDE)]
    for friend in friends:
        pl.semaphore_signal(barrier, inc=1, device_id=friend, device_id_type=MESH)
    snap_rows = pl.ds(pl.multiple_of(core * half, half), half)
    load_snap = pltpu.make_async_copy(snaps, snap.at[snap_rows], small_sem.at[0])
    load_snap.start()
    for k in range(chunks):
        load_own(k).start()
        load_adj(k).start()
    root[...] = jnp.sqrt(volumes[...] * (1.0 / cells))
    acc[...] = jnp.zeros_like(acc)
    acc_snap[...] = jnp.zeros_like(acc_snap)

    pl.semaphore_wait(barrier, len(friends))
    send_snap = remote(snaps, snap.at[snap_rows], ss_sem.at[0], ss_sem.at[1], pair)
    send_snap.start()

    def send_own(k):
        return remote(basis.at[:, piece(k)], other.at[:, piece(k)], bs_sem.at[k], br_sem.at[k], pair)

    for k in range(chunks):
        send_own(k).start()

    def prepare(k, carry):
        cols = piece(k)
        load_own(k).wait()
        left_hi[:tile, cols], left_lo[:tile, cols] = split(own[:, cols] * root[:, cols])
        load_adj(k).wait()
        adj_hi[:, cols], adj_lo[:, cols] = split(adj[:, cols] * root[:, cols])
        return carry

    lax.fori_loop(0, chunks, prepare, 0)
    load_snap.wait()
    send_snap.wait()
    save_snap = pltpu.make_async_copy(snap, snaps_out, out_sem.at[0])
    save_snap.start()
    left_hi[tile:near], left_lo[tile:near] = split(snap[...] * root[...])

    def multiply(k, carry):
        cols = piece(k)
        send_own(k).wait_recv()
        pltpu.make_async_copy(other.at[:, cols], other_out.at[:, cols], out_sem.at[k + 1]).start()
        left_hi[near:, cols], left_lo[near:, cols] = split(other[:, cols] * root[:, cols])
        right = tuple(
            jnp.concatenate([a[:tile, cols], b[:, cols]], axis=0)
            for a, b in ((left_hi, adj_hi), (left_lo, adj_lo))
        )
        acc[...] += dot3((left_hi[:, cols], left_lo[:, cols]), right)
        both = (left_hi[tile:near, cols], left_lo[tile:near, cols])
        acc_snap[...] += dot3(both, both)
        return carry

    lax.fori_loop(0, chunks, multiply, 0)

    mid = tile // 2
    flat = share.shape[1]

    def put(row, value):
        for start in range(0, value.shape[0], flat):
            share[(row + start) // flat] = value[start : start + flat]

    put(0, jnp.concatenate([acc[:mid, :mid], acc[mid:tile, mid:tile]], axis=1))
    snap_square = jnp.concatenate(
        [0.5 * acc_snap[...], jnp.zeros((mid - snap_count, snap_count), f32)], axis=0
    )
    put(
        mid,
        jnp.concatenate(
            [acc[mid:tile, :mid], snap_square, jnp.zeros((mid, mid - snap_count), f32)], axis=1
        ),
    )
    mixed = acc[near:, :tile]
    put(tile, jnp.where(core == 0, mixed[:mid], mixed.T[mid:]))
    put(tile + mid, acc[tile:near, :tile])
    put(tile + mid + snap_count, acc[:tile, tile:])
    put(2 * tile + mid + snap_count, acc[near:, tile:])
    put(3 * tile + mid + snap_count, acc[tile:near, tile:])

    copies = [
        remote(share.at[in_plane(step)], slots.at[step], rs_sem.at[step], rr_sem.at[step],
               plane_peer(step))
        for step in range(1, PLANE)
    ]
    for copy in copies:
        copy.start()
    slots[0] = share[spot]
    for copy in copies:
        copy.wait_recv()
    value = slots[: PLANE // 2] + slots[PLANE // 2 :]
    value = value[: PLANE // 4] + value[PLANE // 4 :]
    value = value[: PLANE // 8] + value[PLANE // 8 :]
    part[0] = value[0] + value[1]

    z_copies = [
        remote(part.at[0], z_slots.at[step], zs_sem.at[step], zr_sem.at[step], level_peer(step))
        for step in range(1, SIDE)
    ]
    for copy in z_copies:
        copy.start()
    for copy in z_copies:
        copy.wait_recv()
    part[1] = (part[0] + z_slots[2]) + (z_slots[1] + z_slots[3])

    g_copies = [
        remote(part.at[1], total.at[0, spot], gs_sem.at[step], gr_sem.at[step], plane_peer(step))
        for step in range(1, PLANE)
    ]
    for copy in g_copies:
        copy.start()
    f_copies = [remote(part.at[1], total.at[1, spot], fs_sem.at[0], fr_sem.at[0], pair)]
    f_copies[0].start()
    total[0, spot] = part[1]
    for step in range(1, PLANE):
        source = in_plane(PLANE - step)
        remote(part.at[1], total.at[0, source], gs_sem.at[step], gr_sem.at[step], pair).wait_recv()
        f_copies.append(
            remote(total.at[0, source], total.at[1, source], fs_sem.at[step], fr_sem.at[step], pair)
        )
        f_copies[-1].start()
    for copy in f_copies:
        copy.wait()
    total_out[...] = total[...]
    for copy in copies + z_copies + g_copies:
        copy.wait_send()

    def finish(k, carry):
        send_own(k).wait_send()
        pltpu.make_async_copy(other.at[:, piece(k)], other_out.at[:, piece(k)], out_sem.at[k + 1]).wait()
        return carry

    lax.fori_loop(0, chunks, finish, 0)
    save_snap.wait()


def gather(cells, basis, adjoint, snapshots, volumes):
    tile, width = basis.shape
    snap_count = 2 * snapshots.shape[0]
    rows = 2 * tile + snap_count
    flat = (7 * tile // 2 + 2 * snap_count) // PLANE
    chunks = width // CHUNK
    dma = pltpu.SemaphoreType.DMA
    vmem = pltpu.VMEM
    any_spec = pl.BlockSpec(memory_space=pl.ANY)
    vmem_spec = pl.BlockSpec(memory_space=vmem)
    return pl.pallas_call(
        functools.partial(gather_kernel, cells),
        out_shape=(
            jax.ShapeDtypeStruct((tile, width), f32),
            jax.ShapeDtypeStruct((snap_count, width), f32),
            jax.ShapeDtypeStruct((2, PLANE, flat, tile), f32),
        ),
        in_specs=[any_spec, any_spec, any_spec, vmem_spec],
        out_specs=(any_spec, any_spec, vmem_spec),
        scratch_shapes=[
            vmem((tile, width), f32),
            vmem((tile, width), f32),
            vmem((tile, width), f32),
            vmem((snap_count, width), f32),
            vmem((1, width), f32),
            vmem((rows, width), bf16),
            vmem((rows, width), bf16),
            vmem((tile, width), bf16),
            vmem((tile, width), bf16),
            vmem((rows, 2 * tile), f32),
            vmem((snap_count, snap_count), f32),
            vmem((PLANE, flat, tile), f32),
            vmem((PLANE, flat, tile), f32),
            vmem((2, flat, tile), f32),
            vmem((SIDE, flat, tile), f32),
            vmem((2, PLANE, flat, tile), f32),
            dma((chunks,)),
            dma((chunks,)),
            dma((1,)),
            dma((chunks,)),
            dma((chunks,)),
            dma((2,)),
            dma((chunks + 1,)),
            dma((PLANE,)),
            dma((PLANE,)),
            dma((SIDE,)),
            dma((SIDE,)),
            dma((PLANE,)),
            dma((PLANE,)),
            dma((PLANE,)),
            dma((PLANE,)),
        ],
        compiler_params=pltpu.CompilerParams(
            collective_id=0, has_side_effects=True, vmem_limit_bytes=56 * 1024 * 1024
        ),
    )(basis, adjoint, snapshots, volumes)


def dot_nn(left, right):
    return lax.dot_general(left, right, (((1,), (0,)), ((), ())), preferred_element_type=f32)


def dot3_nn(left, right):
    rows = left[0].shape[0]
    both = dot_nn(jnp.concatenate([left[0], left[1]], axis=0), right[0])
    return both[:rows] + (dot_nn(left[0], right[1]) + both[rows:])


def exact_tn(left, right):
    return lax.dot_general(
        left, right, (((0,), (0,)), ((), ())), precision=highest, preferred_element_type=f32
    )


def inverse_factor(block, group):
    size = block.shape[0]
    eye = (
        lax.broadcasted_iota(jnp.int32, (size, size), 0)
        == lax.broadcasted_iota(jnp.int32, (size, size), 1)
    ).astype(f32)
    left = jnp.concatenate([block, eye], axis=1)
    done = []
    for start in range(0, size, group):
        count = size - start
        row = lax.broadcasted_iota(jnp.int32, (count, 2 * size), 0)
        cols = [
            jnp.broadcast_to(left[:, start + t : start + t + 1], (count, 2 * size))
            for t in range(group)
        ]
        for t in range(group):
            pivot = cols[t][t : t + 1, :]
            factor = jnp.where(row > t, cols[t], 0.0) * (1.0 / pivot)
            for u in range(t + 1, group):
                cols[u] = cols[u] - factor * cols[u][t : t + 1, :]
            done.append(left[t : t + 1, :] * lax.rsqrt(pivot))
            left = left - factor * left[t : t + 1, :]
        left = left[group:]
    return jnp.concatenate(done, axis=0)[:, size:]


def rotate_kernel(
    basis, other, snaps, total, singular,
    new_out, singular_out, hankel_out,
    rows, result, lead, inverse, coef_hi, coef_lo, in_sem, out_sem,
):
    tile, width = result.shape
    modes = 2 * tile
    snap_count = snaps.shape[0]
    chunks = width // CHUNK
    core = lax.axis_index("mode")
    first_core = core == 0

    def piece(k):
        return pl.ds(pl.multiple_of(k * CHUNK, CHUNK), CHUNK)

    def loads(k):
        cols = piece(k)
        return (
            pltpu.make_async_copy(basis.at[:, cols], rows.at[:tile, cols], in_sem.at[0, k]),
            pltpu.make_async_copy(other.at[:, cols], rows.at[tile:modes, cols], in_sem.at[1, k]),
            pltpu.make_async_copy(snaps.at[:, cols], rows.at[modes:, cols], in_sem.at[2, k]),
        )

    for k in range(chunks):
        for copy in loads(k):
            copy.start()

    s = singular[...]
    s2 = s * s
    mid = tile // 2

    def get(which, row, count):
        flat = total.shape[2]
        first = row // flat
        return total[which, first : first + count // flat].reshape(count, tile)

    def both_cores(row, count):
        mine, others = get(0, row, count), get(1, row, count)
        return jnp.where(first_core, mine, others), jnp.where(first_core, others, mine)

    halves = both_cores(tile + mid, snap_count)
    project_t = jnp.concatenate(halves, axis=1)
    low_diagonal, low_corner = both_cores(0, mid), both_cores(mid, mid)
    snap_square = sum(value[:snap_count, mid : mid + snap_count] for value in low_corner)
    lower = jnp.concatenate(both_cores(tile, mid), axis=0)
    between = exact_nn(halves[1], lower)
    diagonal = jnp.zeros((snap_count, snap_count), f32)
    one_side = exact_nt(between, halves[0])
    for part, ends, corner in zip(halves, low_diagonal, low_corner):
        ahead, behind = part[:, :mid], part[:, mid:]
        diagonal += exact_nt(exact_nn(ahead, ends[:, :mid]), ahead)
        diagonal += exact_nt(exact_nn(behind, ends[:, mid:]), behind)
        one_side += exact_nt(exact_nn(behind, corner[:, :mid]), ahead)
    scaled_t = project_t * s2
    pad = jnp.zeros((tile - 2 * snap_count, modes), f32)
    turned = jnp.concatenate([project_t, scaled_t, pad], axis=0).T
    by_mode, by_mode_scaled = turned[:, :snap_count], turned[:, snap_count : 2 * snap_count]
    inner = (snap_square - exact_nt(project_t, project_t)) + (diagonal + (one_side + one_side.T))
    side = by_mode_scaled + exact_nn(by_mode, inner)
    side_and_project = jnp.concatenate([side, by_mode], axis=1)
    eye = lax.broadcasted_iota(jnp.int32, (modes, modes), 0) == lax.broadcasted_iota(
        jnp.int32, (modes, modes), 1
    )
    lead[...] = jnp.where(eye, s2 * s2, 0.0) + exact_nt(
        side_and_project, turned[:, : 2 * snap_count]
    )
    inverse[...] = eye.astype(f32)
    size = 64
    for start in range(0, modes, size):
        stop = start + size
        small = inverse_factor(lead[start:stop, start:stop], 8)
        part = exact_nn(small, inverse[start:stop, :])
        inverse[start:stop, :] = part
        if stop < modes:
            upper = exact_nn(small, lead[start:stop, :])
            later = upper[:, stop:]
            lead[stop:, :] -= exact_tn(later, upper)
            inverse[stop:, :] -= exact_tn(later, part)

    mine = inverse[pl.ds(pl.multiple_of(core * tile, tile), tile), :]
    both = exact_nn(mine, side_and_project)
    on_snaps = both[:, snap_count:]
    on_modes = mine * s2
    image = (on_modes + exact_nn(on_snaps, project_t)) * s
    energy = exact_nt(jnp.ones((8, modes), f32), image * image) + exact_nt(
        jnp.ones((8, snap_count), f32), both[:, :snap_count] * both[:, :snap_count]
    )
    singular_out[...] = jnp.sqrt(energy[:1])

    on_first, on_second = on_modes[:, :tile], on_modes[:, tile:]
    coef = split(
        jnp.concatenate(
            [
                jnp.where(first_core, on_first, on_second),
                jnp.where(first_core, on_second, on_first),
                on_snaps,
            ],
            axis=1,
        )
    )
    coef_hi[...], coef_lo[...] = coef

    def rotate(k, carry):
        for copy in loads(k):
            copy.wait()
        cols = piece(k)
        result[:, cols] = dot3_nn((coef_hi[...], coef_lo[...]), split(rows[:, cols]))
        pltpu.make_async_copy(result.at[:, cols], new_out.at[:, cols], out_sem.at[k]).start()
        return carry

    lax.fori_loop(0, chunks, rotate, 0)

    base = tile + mid + snap_count
    swapped = (get(1, base + tile, tile), get(1, base, tile), get(1, base + modes, snap_count))
    straight = (get(0, base, tile), get(0, base + tile, tile), get(0, base + modes, snap_count))
    columns = jnp.concatenate(
        [
            jnp.concatenate(
                [jnp.where(first_core, a, b), jnp.where(first_core, b, a)], axis=1
            )
            for a, b in zip(straight, swapped)
        ],
        axis=0,
    )
    hankel_out[...] = dot3_nn(coef, split(columns))

    def finish(k, carry):
        pltpu.make_async_copy(result.at[:, piece(k)], new_out.at[:, piece(k)], out_sem.at[k]).wait()
        return carry

    lax.fori_loop(0, chunks, finish, 0)


def rotate(basis, other, snaps, total, singular):
    tile, width = basis.shape
    modes, snap_count = 2 * tile, snaps.shape[0]
    chunks = width // CHUNK
    dma = pltpu.SemaphoreType.DMA
    vmem = pltpu.VMEM
    any_spec = pl.BlockSpec(memory_space=pl.ANY)
    vmem_spec = pl.BlockSpec(memory_space=vmem)
    return pl.pallas_call(
        rotate_kernel,
        out_shape=(
            jax.ShapeDtypeStruct((tile, width), f32),
            jax.ShapeDtypeStruct((1, tile), f32),
            jax.ShapeDtypeStruct((tile, modes), f32),
        ),
        in_specs=[any_spec] * 3 + [vmem_spec] * 2,
        out_specs=(any_spec, vmem_spec, vmem_spec),
        scratch_shapes=[
            vmem((modes + snap_count, width), f32),
            vmem((tile, width), f32),
            vmem((modes, modes), f32),
            vmem((modes, modes), f32),
            vmem((tile, modes + snap_count), bf16),
            vmem((tile, modes + snap_count), bf16),
            dma((3, chunks)),
            dma((chunks,)),
        ],
        compiler_params=pltpu.CompilerParams(vmem_limit_bytes=56 * 1024 * 1024),
    )(basis, other, snaps, total, singular)


def shards(basis, adjoint, snapshots, volumes, singular):
    tile, width = basis.shape
    cells = float(width * lax.axis_size("space"))
    other, snaps, total = gather(
        cells, basis, adjoint, snapshots, volumes.reshape(1, width)
    )
    new_tile, new_singular, hankel = rotate(
        basis, other, snaps, total, singular.reshape(1, 2 * tile)
    )
    return new_tile, new_singular.reshape(tile), hankel


def solution(mesh):
    return jax.shard_map(
        shards,
        mesh=mesh,
        in_specs=(P("mode", "space"), P("mode", "space"), P("mode", "space"), P("space"), P()),
        out_specs=(P("mode", "space"), P("mode"), P("mode", None)),
        check_vma=False,
    )
```

time: 63.7 us -> 57.5 us (0.903)
  Pallas kernels: 62.9 us -> 56.7 us
    pallas_call x1, Pallas kernels: 44.2 us -> 37.1 us  [gather(): pl.pallas_call(functools.partial(gather_kernel, cells), out_shape=(jax.Sh...]
    pallas_call x1, Pallas kernels: 18.6 us -> 19.6 us  [rotate(): pl.pallas_call(rotate_kernel, out_shape=(jax.ShapeDtypeStruct((tile, widt...]
where the time goes in v3:
time: 57.5 us; the launch traced here: 57.3 us
  Pallas kernels  56.7 us (99%)
  between operations  0.64 us (1%)
    pallas_call x1, Pallas kernels, gather(): pl.pallas_call(functools.partial(gather_kernel, cells), out_shape=(jax.Sh...  37.1 us
    pallas_call x1, Pallas kernels, rotate(): pl.pallas_call(rotate_kernel, out_shape=(jax.ShapeDtypeStruct((tile, widt...  19.6 us

profile of v3, /device:TPU:1, one launch (start us, length us, event | category | flops | bytes accessed | tf_op | source)
XLA Modules:
  0.0 57.3 jit_solution(13453997565289172022)
XLA Ops:
  0.6 37.1 %shard_map.76 = (f32[128,8192]{1,0:T(8,128)}, f32[32,8192]{1,0:T(8,128)}, f32[2,16,32,128]{3,2,1,0:T(8,128)}) custom-call(f32[128,8192]{1,0:T(8,128)} %basis.3, f32[128,8192]{1,0:T(8,128)} %adjoint.1, f32[16,8192]{1,0:T(8,128)} %snaps.1, f32[1,8192]{1,0:T(1,128)} %bitcast.3), custom_call_target="tpu_custom_call" | custom-call | tf_op jit(solution)/shard_map/pallas_call | solution.py:236
  37.8 19.6 %shard_map.77 = (f32[128,8192]{1,0:T(8,128)}, f32[1,128]{1,0:T(1,128)}, f32[128,256]{1,0:T(8,128)}) custom-call(f32[128,8192]{1,0:T(8,128)} %basis.3, f32[128,8192]{1,0:T(8,128)} %get-tuple-element.9.other, f32[32,8192]{1,0:T(8,128)} %get-tuple-element.10.snaps, f32[2,16,32,128]{3,2,1,0:T(8,128)} %get-tuple-element.11.total, f32[1,256]{1,0:T(1,128)} %bitcast.4), custom_call_target="tpu_custom_call" | custom-call | tf_op jit(solution)/shard_map/pallas_call | solution.py:467

commit v4 on v0

v4 whole, which is shorter than its diff:
```python
import functools

import jax
import jax.numpy as jnp
from jax import lax
from jax.experimental import pallas as pl
from jax.experimental.pallas import tpu as pltpu
from jax.sharding import PartitionSpec as P

MESH = pl.DeviceIdType.MESH
highest = lax.Precision.HIGHEST
f32 = jnp.float32
bf16 = jnp.bfloat16
SIDE = 4
PLANE = SIDE * SIDE
CHUNK = 1024


def split(value):
    high = value.astype(bf16)
    return high, (value - high.astype(f32)).astype(bf16)


def dot_nt(left, right):
    return lax.dot_general(left, right, (((1,), (1,)), ((), ())), preferred_element_type=f32)


def dot3(left, right):
    return dot_nt(left[0], right[0]) + (dot_nt(left[0], right[1]) + dot_nt(left[1], right[0]))


def exact_nt(left, right):
    return lax.dot_general(
        left, right, (((1,), (1,)), ((), ())), precision=highest, preferred_element_type=f32
    )


def exact_nn(left, right):
    return lax.dot_general(
        left, right, (((1,), (0,)), ((), ())), precision=highest, preferred_element_type=f32
    )


def dot_nn(left, right):
    return lax.dot_general(left, right, (((1,), (0,)), ((), ())), preferred_element_type=f32)


def dot3_nn(left, right):
    rows = left[0].shape[0]
    both = dot_nn(jnp.concatenate([left[0], left[1]], axis=0), right[0])
    return both[:rows] + (dot_nn(left[0], right[1]) + both[rows:])


def exact_tn(left, right):
    return lax.dot_general(
        left, right, (((0,), (0,)), ((), ())), precision=highest, preferred_element_type=f32
    )


def inverse_factor(block, group):
    size = block.shape[0]
    eye = (
        lax.broadcasted_iota(jnp.int32, (size, size), 0)
        == lax.broadcasted_iota(jnp.int32, (size, size), 1)
    ).astype(f32)
    left = jnp.concatenate([block, eye], axis=1)
    done = []
    for start in range(0, size, group):
        count = size - start
        row = lax.broadcasted_iota(jnp.int32, (count, 2 * size), 0)
        cols = [
            jnp.broadcast_to(left[:, start + t : start + t + 1], (count, 2 * size))
            for t in range(group)
        ]
        for t in range(group):
            pivot = cols[t][t : t + 1, :]
            factor = jnp.where(row > t, cols[t], 0.0) * (1.0 / pivot)
            for u in range(t + 1, group):
                cols[u] = cols[u] - factor * cols[u][t : t + 1, :]
            done.append(left[t : t + 1, :] * lax.rsqrt(pivot))
            left = left - factor * left[t : t + 1, :]
        left = left[group:]
    return jnp.concatenate(done, axis=0)[:, size:]


def factor_kernel(
    cells,
    basis, adjoint, snaps, volumes, singular,
    other_out, snaps_out, coef_out, singular_out, hankel_out,
    own, other, adj, snap, root,
    left_hi, left_lo, adj_hi, adj_lo,
    acc, acc_cross, acc_snap, lead, inverse,
    g_share, g_slots, g_part, g_level, g_total,
    h_share, h_slots, h_part, h_level, h_total,
    load_sem, adj_sem, small_sem, bs_sem, br_sem, ss_sem, out_sem,
    rs_sem, rr_sem, zs_sem, zr_sem, gs_sem, gr_sem, fs_sem, fr_sem,
):
    tile, width = own.shape
    modes = 2 * tile
    mid, low = tile // 2, tile // 4
    snap_count = snap.shape[0]
    half = snap_count // 2
    chunks = width // CHUNK
    near = tile + snap_count
    place = lax.axis_index("space")
    core = lax.axis_index("mode")
    first_core = core == 0
    pair = (place, 1 - core)
    spot = lax.rem(place, PLANE)
    level = place // PLANE

    def in_plane(step):
        return lax.rem(spot + step, PLANE)

    def plane_peer(step):
        return (level * PLANE + in_plane(step), core)

    def level_peer(step):
        return (lax.rem(level + step, SIDE) * PLANE + spot, core)

    def piece(k):
        return pl.ds(pl.multiple_of(k * CHUNK, CHUNK), CHUNK)

    def load_own(k):
        return pltpu.make_async_copy(basis.at[:, piece(k)], own.at[:, piece(k)], load_sem.at[k])

    def load_adj(k):
        return pltpu.make_async_copy(adjoint.at[:, piece(k)], adj.at[:, piece(k)], adj_sem.at[k])

    def remote(src, dst, send_sem, recv_sem, device):
        return pltpu.make_async_remote_copy(
            src_ref=src, dst_ref=dst, send_sem=send_sem, recv_sem=recv_sem,
            device_id=device, device_id_type=MESH,
        )

    barrier = pltpu.get_barrier_semaphore()
    friends = [pair]
    friends += [plane_peer(step) for step in range(1, PLANE)]
    friends += [level_peer(step) for step in range(1, SIDE)]
    for friend in friends:
        pl.semaphore_signal(barrier, inc=1, device_id=friend, device_id_type=MESH)
    snap_rows = pl.ds(pl.multiple_of(core * half, half), half)
    load_snap = pltpu.make_async_copy(snaps, snap.at[snap_rows], small_sem.at[0])
    load_snap.start()
    for k in range(chunks):
        load_own(k).start()
    for k in range(chunks):
        load_adj(k).start()
    root[...] = jnp.sqrt(volumes[...] * (1.0 / cells))
    for ref in (acc, acc_cross, acc_snap, h_share):
        ref[...] = jnp.zeros_like(ref)

    pl.semaphore_wait(barrier, len(friends))
    send_snap = remote(snaps, snap.at[snap_rows], ss_sem.at[0], ss_sem.at[1], pair)
    send_snap.start()

    def send_own(k):
        return remote(basis.at[:, piece(k)], other.at[:, piece(k)], bs_sem.at[k], br_sem.at[k], pair)

    def turn(k, which):
        return lax.rem(k + which * (chunks // 2), chunks)

    for k in range(chunks):
        send_own(turn(k, 1 - core)).start()

    def prepare(k, carry):
        cols = piece(k)
        load_own(k).wait()
        left_hi[:tile, cols], left_lo[:tile, cols] = split(own[:, cols] * root[:, cols])
        return carry

    lax.fori_loop(0, chunks, prepare, 0)
    load_snap.wait()
    send_snap.wait()
    save_snap = pltpu.make_async_copy(snap, snaps_out, out_sem.at[0])
    save_snap.start()
    left_hi[tile:near], left_lo[tile:near] = split(snap[...] * root[...])

    def multiply_own(k, carry):
        cols = piece(k)
        right = (left_hi[:tile, cols], left_lo[:tile, cols])
        acc[:near] += dot3((left_hi[:near, cols], left_lo[:near, cols]), right)
        both = (left_hi[tile:near, cols], left_lo[tile:near, cols])
        acc_snap[...] += dot3(both, both)
        return carry

    lax.fori_loop(0, chunks, multiply_own, 0)

    def arrive(k):
        cols = piece(k)
        send_own(k).wait_recv()
        pltpu.make_async_copy(other.at[:, cols], other_out.at[:, cols], out_sem.at[k + 1]).start()
        left_hi[near:, cols], left_lo[near:, cols] = split(other[:, cols] * root[:, cols])
        return cols

    def multiply_other(step, carry):
        cols = arrive(turn(step, core))
        acc[near:] += dot3(
            (left_hi[near:, cols], left_lo[near:, cols]), (left_hi[:tile, cols], left_lo[:tile, cols])
        )
        return carry

    lax.fori_loop(0, chunks // 2, multiply_other, 0)

    def put(row, value):
        flat = g_share.shape[1]
        for start in range(0, value.shape[0], flat):
            g_share[(row + start) // flat] = value[start : start + flat]

    ahead = jnp.concatenate(
        [jnp.concatenate([acc[:low, :low], 0.5 * acc_snap[...]], axis=1), acc[low:mid, :mid]], axis=0
    )
    put(0, jnp.concatenate([ahead, acc[mid:tile, mid:tile]], axis=1))
    by_snap = acc[tile:near, :tile]
    put(
        mid,
        jnp.concatenate(
            [acc[mid:tile, :mid], jnp.concatenate([by_snap[:, :mid], by_snap[:, mid:]], axis=0)], axis=1
        ),
    )
    mixed = acc[near:, :]
    put(tile, jnp.where(first_core, mixed, mixed.T))

    def scatter(group, share, slots):
        copies = [
            remote(share.at[in_plane(step)], slots.at[step], rs_sem.at[group, step],
                   rr_sem.at[group, step], plane_peer(step))
            for step in range(1, PLANE)
        ]
        for copy in copies:
            copy.start()
        slots[0] = share[spot]
        return copies

    def exchange(group, copies, slots, part, levels):
        for copy in copies:
            copy.wait()
        value = slots[: PLANE // 2] + slots[PLANE // 2 :]
        value = value[: PLANE // 4] + value[PLANE // 4 :]
        value = value[: PLANE // 8] + value[PLANE // 8 :]
        part[0] = value[0] + value[1]
        copies = [
            remote(part.at[0], levels.at[step], zs_sem.at[group, step], zr_sem.at[group, step],
                   level_peer(step))
            for step in range(1, SIDE)
        ]
        for copy in copies:
            copy.start()
        return copies

    def spread(group, copies, part, levels, total):
        for copy in copies:
            copy.wait()
        part[1] = (part[0] + levels[2]) + (levels[1] + levels[3])
        copies = [
            remote(part.at[1], total.at[0, spot], gs_sem.at[group, step], gr_sem.at[group, step],
                   plane_peer(step))
            for step in range(1, PLANE)
        ]
        passed = [remote(part.at[1], total.at[1, spot], fs_sem.at[group, 0], fr_sem.at[group, 0], pair)]
        for copy in copies + passed:
            copy.start()
        total[0, spot] = part[1]
        return copies, passed

    def pass_on(group, copies, passed, part, total):
        for step in range(1, PLANE):
            source = in_plane(PLANE - step)
            remote(part.at[1], total.at[0, source], gs_sem.at[group, step], gr_sem.at[group, step],
                   pair).wait_recv()
            passed.append(
                remote(total.at[0, source], total.at[1, source], fs_sem.at[group, step],
                       fr_sem.at[group, step], pair)
            )
            passed[-1].start()
        for copy in copies:
            copy.wait_send()
        return passed

    copies = scatter(0, g_share, g_slots)

    def adjoint_own(k, carry):
        cols = piece(k)
        load_adj(k).wait()
        right = split(adj[:, cols] * root[:, cols])
        adj_hi[:, cols], adj_lo[:, cols] = right
        acc_cross[:near] += dot3((left_hi[:near, cols], left_lo[:near, cols]), right)
        return carry

    def adjoint_other(k, carry):
        cols = piece(k)
        acc_cross[near:] += dot3(
            (left_hi[near:, cols], left_lo[near:, cols]), (adj_hi[:, cols], adj_lo[:, cols])
        )
        return carry

    def rest(step, carry):
        arrive(turn(step, core))
        return carry

    lax.fori_loop(0, chunks, adjoint_own, 0)
    copies = exchange(0, copies, g_slots, g_part, g_level)
    lax.fori_loop(chunks // 2, chunks, rest, 0)
    lax.fori_loop(0, chunks, adjoint_other, 0)
    copies, passed = spread(0, copies, g_part, g_level, g_total)
    flat = h_share.shape[1]
    count = (modes + snap_count) // flat
    h_share[:count] = acc_cross[...].reshape(count, flat, tile)
    h_copies = scatter(1, h_share, h_slots)
    for copy in pass_on(0, copies, passed, g_part, g_total):
        copy.wait()

    def get(which, row, rows):
        size = g_total.shape[2]
        return g_total[which, row // size : (row + rows) // size].reshape(rows, tile)

    def by_core(mine, others):
        return jnp.where(first_core, mine, others), jnp.where(first_core, others, mine)

    s = singular[...]
    s2 = s * s
    tops = by_core(get(0, 0, mid), get(1, 0, mid))
    bottoms = by_core(get(0, mid, mid), get(1, mid, mid))
    lower = get(0, tile, tile) + get(1, tile, tile)
    halves = [
        jnp.concatenate([value[:low, mid:], value[low:, mid:]], axis=1) for value in bottoms
    ]
    project_t = jnp.concatenate(halves, axis=1)
    snap_square = tops[0][:low, low:mid] + tops[1][:low, low:mid]
    one_side = exact_nt(exact_nn(halves[1], lower), halves[0])
    diagonal = snap_square - exact_nt(project_t, project_t)
    for part, top, bottom in zip(halves, tops, bottoms):
        ahead, behind = part[:, :mid], part[:, mid:]
        ends = jnp.concatenate(
            [jnp.concatenate([top[:low, :low], top[low:, :low].T], axis=1), top[low:, :mid]], axis=0
        )
        diagonal += exact_nt(exact_nn(ahead, ends), ahead)
        diagonal += exact_nt(exact_nn(behind, top[:, mid:]), behind)
        one_side += exact_nt(exact_nn(behind, bottom[:, :mid]), ahead)
    inner = diagonal + (one_side + one_side.T)

    pad = jnp.zeros((tile - 2 * snap_count, modes), f32)
    turned = jnp.concatenate([project_t, project_t * s2, pad], axis=0).T
    by_mode, by_mode_scaled = turned[:, :snap_count], turned[:, snap_count : 2 * snap_count]
    side = by_mode_scaled + exact_nn(by_mode, inner)
    side_and_project = jnp.concatenate([side, by_mode], axis=1)
    eye = lax.broadcasted_iota(jnp.int32, (modes, modes), 0) == lax.broadcasted_iota(
        jnp.int32, (modes, modes), 1
    )
    lead[...] = jnp.where(eye, s2 * s2, 0.0) + exact_nt(
        side_and_project, turned[:, : 2 * snap_count]
    )
    inverse[...] = eye.astype(f32)
    size = 64
    for start in range(0, modes, size):
        stop = start + size
        small = inverse_factor(lead[start:stop, start:stop], 8)
        part = exact_nn(small, inverse[start:stop, :])
        inverse[start:stop, :] = part
        if stop < modes:
            upper = exact_nn(small, lead[start:stop, :])
            later = upper[:, stop:]
            lead[stop:, :] -= exact_tn(later, upper)
            inverse[stop:, :] -= exact_tn(later, part)
        if start == 0:
            h_copies = exchange(1, h_copies, h_slots, h_part, h_level)
        elif start == size:
            h_copies, h_passed = spread(1, h_copies, h_part, h_level, h_total)
        elif start == 2 * size:
            h_passed = pass_on(1, h_copies, h_passed, h_part, h_total)

    mine = inverse[pl.ds(pl.multiple_of(core * tile, tile), tile), :]
    both = exact_nn(mine, side_and_project)
    on_snaps = both[:, snap_count:]
    on_modes = mine * s2
    image = (on_modes + exact_nn(on_snaps, project_t)) * s
    energy = exact_nt(jnp.ones((8, modes), f32), image * image) + exact_nt(
        jnp.ones((8, snap_count), f32), both[:, :snap_count] * both[:, :snap_count]
    )
    singular_out[...] = jnp.sqrt(energy[:1])
    on_own, on_other = by_core(on_modes[:, :tile], on_modes[:, tile:])
    coef = jnp.concatenate([on_own, on_other, on_snaps], axis=1)
    coef_out[...] = coef

    for copy in h_passed:
        copy.wait()
    straight = h_total[0, :count].reshape(count * flat, tile)
    swapped = h_total[1, :count].reshape(count * flat, tile)
    swapped = jnp.concatenate([swapped[near:], swapped[tile:near], swapped[:tile]], axis=0)
    columns = jnp.concatenate(by_core(straight, swapped), axis=1)
    columns = jnp.concatenate([columns[:tile], columns[near:], columns[tile:near]], axis=0)
    hankel_out[...] = dot3_nn(split(coef), split(columns))

    def finish(k, carry):
        send_own(k).wait_send()
        pltpu.make_async_copy(other.at[:, piece(k)], other_out.at[:, piece(k)], out_sem.at[k + 1]).wait()
        return carry

    lax.fori_loop(0, chunks, finish, 0)
    save_snap.wait()


def factor(cells, basis, adjoint, snapshots, volumes, singular):
    tile, width = basis.shape
    snap_count = 2 * snapshots.shape[0]
    modes = 2 * tile
    rows = modes + snap_count
    chunks = width // CHUNK
    dma = pltpu.SemaphoreType.DMA
    vmem = pltpu.VMEM
    any_spec = pl.BlockSpec(memory_space=pl.ANY)
    vmem_spec = pl.BlockSpec(memory_space=vmem)

    def sums(flat):
        return [
            vmem((PLANE, flat, tile), f32),
            vmem((PLANE, flat, tile), f32),
            vmem((2, flat, tile), f32),
            vmem((SIDE, flat, tile), f32),
            vmem((2, PLANE, flat, tile), f32),
        ]

    return pl.pallas_call(
        functools.partial(factor_kernel, cells),
        out_shape=(
            jax.ShapeDtypeStruct((tile, width), f32),
            jax.ShapeDtypeStruct((snap_count, width), f32),
            jax.ShapeDtypeStruct((tile, rows), f32),
            jax.ShapeDtypeStruct((1, tile), f32),
            jax.ShapeDtypeStruct((tile, modes), f32),
        ),
        in_specs=[any_spec, any_spec, any_spec, vmem_spec, vmem_spec],
        out_specs=(any_spec, any_spec, vmem_spec, vmem_spec, vmem_spec),
        scratch_shapes=[
            vmem((tile, width), f32),
            vmem((tile, width), f32),
            vmem((tile, width), f32),
            vmem((snap_count, width), f32),
            vmem((1, width), f32),
            vmem((rows, width), bf16),
            vmem((rows, width), bf16),
            vmem((tile, width), bf16),
            vmem((tile, width), bf16),
            vmem((rows, tile), f32),
            vmem((rows, tile), f32),
            vmem((snap_count, snap_count), f32),
            vmem((modes, modes), f32),
            vmem((modes, modes), f32),
            *sums(16),
            *sums(24),
            dma((chunks,)),
            dma((chunks,)),
            dma((1,)),
            dma((chunks,)),
            dma((chunks,)),
            dma((2,)),
            dma((chunks + 1,)),
            dma((2, PLANE)),
            dma((2, PLANE)),
            dma((2, SIDE)),
            dma((2, SIDE)),
            dma((2, PLANE)),
            dma((2, PLANE)),
            dma((2, PLANE)),
            dma((2, PLANE)),
        ],
        compiler_params=pltpu.CompilerParams(
            collective_id=0, has_side_effects=True, vmem_limit_bytes=56 * 1024 * 1024
        ),
    )(basis, adjoint, snapshots, volumes, singular)


def rotate_kernel(basis, other, snaps, coef, new_out, rows, result, in_sem, out_sem):
    tile, width = result.shape
    modes = 2 * tile
    chunks = width // CHUNK

    def piece(k):
        return pl.ds(pl.multiple_of(k * CHUNK, CHUNK), CHUNK)

    def loads(k):
        cols = piece(k)
        return (
            pltpu.make_async_copy(basis.at[:, cols], rows.at[:tile, cols], in_sem.at[0, k]),
            pltpu.make_async_copy(other.at[:, cols], rows.at[tile:modes, cols], in_sem.at[1, k]),
            pltpu.make_async_copy(snaps.at[:, cols], rows.at[modes:, cols], in_sem.at[2, k]),
        )

    for k in range(chunks):
        for copy in loads(k):
            copy.start()
    parts = split(coef[...])

    def step(k, carry):
        for copy in loads(k):
            copy.wait()
        cols = piece(k)
        result[:, cols] = dot3_nn(parts, split(rows[:, cols]))
        pltpu.make_async_copy(result.at[:, cols], new_out.at[:, cols], out_sem.at[k]).start()
        return carry

    lax.fori_loop(0, chunks, step, 0)

    def finish(k, carry):
        pltpu.make_async_copy(result.at[:, piece(k)], new_out.at[:, piece(k)], out_sem.at[k]).wait()
        return carry

    lax.fori_loop(0, chunks, finish, 0)


def rotate(basis, other, snaps, coef):
    tile, width = basis.shape
    chunks = width // CHUNK
    dma = pltpu.SemaphoreType.DMA
    any_spec = pl.BlockSpec(memory_space=pl.ANY)
    return pl.pallas_call(
        rotate_kernel,
        out_shape=jax.ShapeDtypeStruct((tile, width), f32),
        in_specs=[any_spec] * 3 + [pl.BlockSpec(memory_space=pltpu.VMEM)],
        out_specs=any_spec,
        scratch_shapes=[
            pltpu.VMEM((coef.shape[1], width), f32),
            pltpu.VMEM((tile, width), f32),
            dma((3, chunks)),
            dma((chunks,)),
        ],
        compiler_params=pltpu.CompilerParams(vmem_limit_bytes=56 * 1024 * 1024),
    )(basis, other, snaps, coef)


def shards(basis, adjoint, snapshots, volumes, singular):
    tile, width = basis.shape
    cells = float(width * lax.axis_size("space"))
    other, snaps, coef, new_singular, hankel = factor(
        cells, basis, adjoint, snapshots, volumes.reshape(1, width), singular.reshape(1, 2 * tile)
    )
    return rotate(basis, other, snaps, coef), new_singular.reshape(tile), hankel


def solution(mesh):
    return jax.shard_map(
        shards,
        mesh=mesh,
        in_specs=(P("mode", "space"), P("mode", "space"), P("mode", "space"), P("space"), P()),
        out_specs=(P("mode", "space"), P("mode"), P("mode", None)),
        check_vma=False,
    )
```

time: 1020 us -> 63.9 us (0.06)
  blocking collectives: 590 us -> 0 us
  waiting for transfers between devices: 292 us -> 0 us
  other arithmetic: 63.3 us -> 0 us
  Pallas kernels: 0 us -> 61.7 us
  matrix products: 49.6 us -> 0 us
  between operations: 15.6 us -> 0.67 us
    psum x2 -> x0, blocking collectives: 588 us -> none  [the longest x1 294 us: shards(): project_tile = lax.psum(project_tile, 'space')]
    reduce_scatter x2 -> x0, waiting for transfers between devices: 123 us -> none  [shards(): lax.psum_scatter(jnp.dot(part_cols.T, basis, precision=highest), 'mode',...]
    psum x1 -> x0, waiting for transfers between devices: 121 us -> none  [shards(): lax.psum(jnp.dot(new_tile * scaled, adjoint_full.T, precision=highest), '...]
    pallas_call x0 -> x2, Pallas kernels: none -> 61.7 us  [the longest x1 53.8 us: factor(): pl.pallas_call(functools.partial(factor_kernel, cells), out_shape=(jax.Sh...]
    another operation x14 -> x0, other arithmetic: 60.5 us -> none  [the longest x6 34.1 us: truncate(): jnp.linalg.cholesky(jnp.dot(leading.T, leading, precision=highest))]
    dot_general x11 -> x0, matrix products: 48 us -> none  [the longest x2 16 us: shards(): jnp.dot(part_cols.T, basis, precision=highest)]
    all_gather x3 -> x0, waiting for transfers between devices: 46.7 us -> none  [the longest x1 18.9 us: shards(): adjoint_full = lax.all_gather(adjoint, 'mode', axis=0, tiled=True)]
  transfers between devices with their start and end apart: 6 -> 0, of which waited for: 6 -> 0; matrix products, arithmetic and copies ran while one was open for 1% -> 0% of each run, Pallas kernels for 0% -> 0%
where the time goes in v4:
time: 63.9 us; the launch traced here: 63.5 us
  Pallas kernels  61.7 us (97%)
  local copies, waits for them, and re-layouts  1.18 us (2%)
  between operations  0.67 us (1%)
    pallas_call x1, Pallas kernels, factor(): pl.pallas_call(functools.partial(factor_kernel, cells), out_shape=(jax.Sh...  53.8 us
    pallas_call x1, Pallas kernels, rotate(): pl.pallas_call(rotate_kernel, out_shape=jax.ShapeDtypeStruct((tile, width...  7.88 us

profile of v4, /device:TPU:1, one launch (start us, length us, event | category | flops | bytes accessed | tf_op | source)
XLA Modules:
  0.0 63.5 jit_solution(1592215595870804894)
XLA Ops:
  0.6 53.8 %shard_map.76 = (f32[128,8192]{1,0:T(8,128)}, f32[32,8192]{1,0:T(8,128)}, f32[128,288]{1,0:T(8,128)}, f32[1,128]{1,0:T(1,128)}, f32[128,256]{1,0:T(8,128)}) custom-call(f32[128,8192]{1,0:T(8,128)} %basis.3, f32[128,8192]{1,0:T(8,128)} %adjoint.1, f32[16,8192]{1,0:T(8,128)} %snaps.1, f32[1,8192]{1,0:T(1,128)} %bitcast.3, f32[1,256]{1,0:T(1,128)} %bitcast.4), custom_call_target="tpu_custom_call" | custom-call | tf_op jit(solution)/shard_map/pallas_call | solution.py:423
  54.4 0.0 copy-start.1
  54.4 0.0 copy-start
  54.4 7.9 %shard_map.77 = f32[128,8192]{1,0:T(8,128)} custom-call(f32[128,8192]{1,0:T(8,128)} %basis.3, f32[128,8192]{1,0:T(8,128)} %get-tuple-element.8.other, f32[32,8192]{1,0:T(8,128)} %get-tuple-element.9.snaps, f32[128,288]{1,0:T(8,128)} %get-tuple-element.10.coef), custom_call_target="tpu_custom_call" | custom-call | tf_op jit(solution)/shard_map/pallas_call | solution.py:516
  62.3 0.0 copy-done.1
  62.3 0.5 copy.10
  62.9 0.0 copy-done
  62.9 0.7 %copy.11 = f32[128,256]{1,0:T(8,128)} copy(f32[128,256]{1,0:T(8,128)S(1)} %copy-done) | data formatting | bytes 262144
Async XLA Ops:
  54.4 7.9 %copy-start.1 = (f32[1,128]{1,0:T(1,128)S(1)}, f32[1,128]{1,0:T(1,128)}, u32[]{:S(2)}) copy-start(f32[1,128]{1,0:T(1,128)} %get-tuple-element.11) | copy-start | bytes 1540
  54.4 8.4 %copy-start = (f32[128,256]{1,0:T(8,128)S(1)}, f32[128,256]{1,0:T(8,128)}, u32[]{:S(2)}) copy-start(f32[128,256]{1,0:T(8,128)} %get-tuple-element.18) | copy-start | bytes 393220

commit v5 on v3

--- a/solution.py
+++ b/solution.py
@@ -44,7 +44,7 @@
 def gather_kernel(
     cells,
     basis, adjoint, snaps, volumes,
-    other_out, snaps_out, total_out,
+    hi_out, lo_out, total_out,
     own, other, adj, snap, root,
     left_hi, left_lo, adj_hi, adj_lo,
     acc, acc_snap, share, slots, part, z_slots, total,
@@ -123,15 +123,21 @@
     lax.fori_loop(0, chunks, prepare, 0)
     load_snap.wait()
     send_snap.wait()
-    save_snap = pltpu.make_async_copy(snap, snaps_out, out_sem.at[0])
-    save_snap.start()
     left_hi[tile:near], left_lo[tile:near] = split(snap[...] * root[...])
+
+    def saves(k):
+        cols = piece(k)
+        return (
+            pltpu.make_async_copy(left_hi.at[:, cols], hi_out.at[:, cols], out_sem.at[0, k]),
+            pltpu.make_async_copy(left_lo.at[:, cols], lo_out.at[:, cols], out_sem.at[1, k]),
+        )
 
     def multiply(k, carry):
         cols = piece(k)
         send_own(k).wait_recv()
-        pltpu.make_async_copy(other.at[:, cols], other_out.at[:, cols], out_sem.at[k + 1]).start()
         left_hi[near:, cols], left_lo[near:, cols] = split(other[:, cols] * root[:, cols])
+        for copy in saves(k):
+            copy.start()
         right = tuple(
             jnp.concatenate([a[:tile, cols], b[:, cols]], axis=0)
             for a, b in ((left_hi, adj_hi), (left_lo, adj_lo))
@@ -216,11 +222,11 @@
 
     def finish(k, carry):
         send_own(k).wait_send()
-        pltpu.make_async_copy(other.at[:, piece(k)], other_out.at[:, piece(k)], out_sem.at[k + 1]).wait()
+        for copy in saves(k):
+            copy.wait()
         return carry
 
     lax.fori_loop(0, chunks, finish, 0)
-    save_snap.wait()
 
 
 def gather(cells, basis, adjoint, snapshots, volumes):
@@ -236,8 +242,8 @@
     return pl.pallas_call(
         functools.partial(gather_kernel, cells),
         out_shape=(
-            jax.ShapeDtypeStruct((tile, width), f32),
-            jax.ShapeDtypeStruct((snap_count, width), f32),
+            jax.ShapeDtypeStruct((rows, width), bf16),
+            jax.ShapeDtypeStruct((rows, width), bf16),
             jax.ShapeDtypeStruct((2, PLANE, flat, tile), f32),
         ),
         in_specs=[any_spec, any_spec, any_spec, vmem_spec],
@@ -265,7 +271,7 @@
             dma((chunks,)),
             dma((chunks,)),
             dma((2,)),
-            dma((chunks + 1,)),
+            dma((2, chunks)),
             dma((PLANE,)),
             dma((PLANE,)),
             dma((SIDE,)),
@@ -297,40 +303,151 @@
     )
 
 
-def inverse_factor(block, group):
-    size = block.shape[0]
+def inverse_factors(blocks, group):
+    size = blocks[0].shape[0]
+    width = 2 * size
     eye = (
         lax.broadcasted_iota(jnp.int32, (size, size), 0)
         == lax.broadcasted_iota(jnp.int32, (size, size), 1)
     ).astype(f32)
-    left = jnp.concatenate([block, eye], axis=1)
-    done = []
+    lefts = [jnp.concatenate([block, eye], axis=1) for block in blocks]
+    done = [[] for _ in blocks]
     for start in range(0, size, group):
         count = size - start
-        row = lax.broadcasted_iota(jnp.int32, (count, 2 * size), 0)
+        row = lax.broadcasted_iota(jnp.int32, (count, width), 0)
         cols = [
-            jnp.broadcast_to(left[:, start + t : start + t + 1], (count, 2 * size))
-            for t in range(group)
+            [
+                jnp.broadcast_to(left[:, start + t : start + t + 1], (count, width))
+                for t in range(group)
+            ]
+            for left in lefts
         ]
         for t in range(group):
-            pivot = cols[t][t : t + 1, :]
-            factor = jnp.where(row > t, cols[t], 0.0) * (1.0 / pivot)
-            for u in range(t + 1, group):
-                cols[u] = cols[u] - factor * cols[u][t : t + 1, :]
-            done.append(left[t : t + 1, :] * lax.rsqrt(pivot))
-            left = left - factor * left[t : t + 1, :]
-        left = left[group:]
-    return jnp.concatenate(done, axis=0)[:, size:]
+            for n, col in enumerate(cols):
+                pivot = col[t][t : t + 1, :]
+                factor = jnp.where(row > t, col[t], 0.0) * (1.0 / pivot)
+                for u in range(t + 1, group):
+                    col[u] = col[u] - factor * col[u][t : t + 1, :]
+                done[n].append(lefts[n][t : t + 1, :] * lax.rsqrt(pivot))
+                lefts[n] = lefts[n] - factor * lefts[n][t : t + 1, :]
+        lefts = [left[group:] for left in lefts]
+    return [jnp.concatenate(rows, axis=0)[:, size:] for rows in done]
+
+
+def paired_inverses(blocks, group):
+    size = blocks[0].shape[0]
+    half, width = size // 2, 2 * size
+    eye = (
+        lax.broadcasted_iota(jnp.int32, (size, size), 0)
+        == lax.broadcasted_iota(jnp.int32, (size, size), 1)
+    ).astype(f32)
+    lefts = [jnp.concatenate([block, eye], axis=1) for block in blocks]
+    row = lax.broadcasted_iota(jnp.int32, (size, width), 0)
+    row = jnp.where(row >= half, row - half, row)
+    entries = [([], [], []) for _ in blocks]
+    for start in range(0, half, group):
+        places = list(range(start, start + group)) + list(range(half + start, half + start + group))
+        cols = [
+            [jnp.broadcast_to(left[:, at : at + 1], (size, width)) for at in places] for left in lefts
+        ]
+        for t in range(group):
+            at = start + t
+            upper, lower = slice(at, at + 1), slice(half + at, half + at + 1)
+            below = row > at
+            for n, col in enumerate(cols):
+                first, second = col[t], col[group + t]
+                alpha, beta, delta = first[upper], second[upper], second[lower]
+                scale = 1.0 / (alpha * delta - beta * beta)
+                a, b, c = delta * scale, -(beta * scale), alpha * scale
+                for kept, value in zip(entries[n], (a, b, c)):
+                    kept.append(value)
+                on_upper = jnp.where(below, first * a + second * b, 0.0)
+                on_lower = jnp.where(below, first * b + second * c, 0.0)
+                for u in list(range(t + 1, group)) + list(range(group + t + 1, 2 * group)):
+                    col[u] = col[u] - (on_upper * col[u][upper] + on_lower * col[u][lower])
+                lefts[n] = lefts[n] - (on_upper * lefts[n][upper] + on_lower * lefts[n][lower])
+    return [
+        (left[:, size:], [jnp.concatenate(kept, axis=0) for kept in kinds])
+        for left, kinds in zip(lefts, entries)
+    ]
+
+
+def own_inverse(project_t, s2, gram, first_core):
+    snap_count, modes = project_t.shape
+    tile, size = modes // 2, 64
+    lane = lax.broadcasted_iota(jnp.int32, (1, modes), 1)
+    offset = jnp.where(first_core, 0, tile)
+    s4 = s2 * s2
+    joined = jnp.concatenate([project_t * s2, project_t], axis=0)
+    over2, over4 = project_t / s2, project_t / s4
+    eye = (
+        lax.broadcasted_iota(jnp.int32, (snap_count, snap_count), 0)
+        == lax.broadcasted_iota(jnp.int32, (snap_count, snap_count), 1)
+    ).astype(f32)
+    diagonal = (
+        lax.broadcasted_iota(jnp.int32, (tile, tile), 0)
+        == lax.broadcasted_iota(jnp.int32, (tile, tile), 1)
+    )
+    own_s4 = jnp.where(first_core, s4[:, :tile], s4[:, tile:])
+    own_diagonal = jnp.where(diagonal, own_s4, 0.0)
+    row = lax.broadcasted_iota(jnp.int32, (size, modes), 0)
+    starts = list(range(0, tile, size))
+    befores = [lane < offset + start for start in starts]
+    stack = jnp.concatenate(
+        [
+            part
+            for before in befores
+            for part in (
+                jnp.where(before, over2, 0.0),
+                jnp.where(before, over4, 0.0),
+                jnp.where(before, 0.0, project_t),
+            )
+        ],
+        axis=0,
+    )
+    sums = exact_nt(stack, project_t)
+    blocks = []
+    for n in range(len(starts)):
+        at2, at4, after = (
+            sums[(3 * n + m) * snap_count : (3 * n + m + 1) * snap_count] for m in range(3)
+        )
+        blocks.append(
+            jnp.concatenate(
+                [
+                    jnp.concatenate([-(after + gram), at2 + eye], axis=1),
+                    jnp.concatenate([at2 + eye, at4], axis=1),
+                ],
+                axis=0,
+            )
+        )
+    lefts, rests = [], []
+    for start, before, (change, entries) in zip(starts, befores, paired_inverses(blocks, 4)):
+        image = exact_nn(change, joined)
+        top, bottom = image[:snap_count], image[snap_count:]
+        a, b, c = (jnp.broadcast_to(value[:, :1], top.shape) for value in entries)
+        solved = jnp.concatenate([a * top + b * bottom, b * top + c * bottom], axis=0)
+        stop = start + size
+        mine = jnp.where(first_core, image[:, :tile], image[:, tile:])[:, start:stop]
+        solved_mine = jnp.where(first_core, solved[:, :tile], solved[:, tile:])[:, start:stop]
+        lefts.append(own_diagonal[start:stop, start:stop] + exact_tn(mine, solved_mine))
+        rests.append(
+            (lane == offset + start + row).astype(f32)
+            - exact_tn(mine, jnp.where(before, solved / s4, 0.0))
+        )
+    smalls = inverse_factors(lefts, 8)
+    return jnp.concatenate([exact_nn(small, rest) for small, rest in zip(smalls, rests)], axis=0)
 
 
 def rotate_kernel(
-    basis, other, snaps, total, singular,
+    cells,
+    hi, lo, total, singular, volumes,
     new_out, singular_out, hankel_out,
-    rows, result, lead, inverse, coef_hi, coef_lo, in_sem, out_sem,
+    rows_hi, rows_lo, result, root, in_sem, out_sem,
 ):
     tile, width = result.shape
     modes = 2 * tile
-    snap_count = snaps.shape[0]
+    snap_count = hi.shape[0] - modes
+    near = tile + snap_count
     chunks = width // CHUNK
     core = lax.axis_index("mode")
     first_core = core == 0
@@ -341,14 +458,14 @@
     def loads(k):
         cols = piece(k)
         return (
-            pltpu.make_async_copy(basis.at[:, cols], rows.at[:tile, cols], in_sem.at[0, k]),
-            pltpu.make_async_copy(other.at[:, cols], rows.at[tile:modes, cols], in_sem.at[1, k]),
-            pltpu.make_async_copy(snaps.at[:, cols], rows.at[modes:, cols], in_sem.at[2, k]),
+            pltpu.make_async_copy(hi.at[:, cols], rows_hi.at[:, cols], in_sem.at[0, k]),
+            pltpu.make_async_copy(lo.at[:, cols], rows_lo.at[:, cols], in_sem.at[1, k]),
         )
 
     for k in range(chunks):
         for copy in loads(k):
             copy.start()
+    root[...] = lax.rsqrt(volumes[...] * (1.0 / cells))
 
     s = singular[...]
     s2 = s * s
@@ -380,29 +497,14 @@
     pad = jnp.zeros((tile - 2 * snap_count, modes), f32)
     turned = jnp.concatenate([project_t, scaled_t, pad], axis=0).T
     by_mode, by_mode_scaled = turned[:, :snap_count], turned[:, snap_count : 2 * snap_count]
-    inner = (snap_square - exact_nt(project_t, project_t)) + (diagonal + (one_side + one_side.T))
-    side = by_mode_scaled + exact_nn(by_mode, inner)
+    square = exact_nt(project_t, project_t)
+    gram = (snap_square - 2.0 * square) + (diagonal + (one_side + one_side.T))
+    pad = jnp.zeros((tile - 2 * snap_count, modes), f32)
+    turned = jnp.concatenate([project_t, project_t * s2, pad], axis=0).T
+    by_mode, by_mode_scaled = turned[:, :snap_count], turned[:, snap_count : 2 * snap_count]
+    side = by_mode_scaled + exact_nn(by_mode, square + gram)
     side_and_project = jnp.concatenate([side, by_mode], axis=1)
-    eye = lax.broadcasted_iota(jnp.int32, (modes, modes), 0) == lax.broadcasted_iota(
-        jnp.int32, (modes, modes), 1
-    )
-    lead[...] = jnp.where(eye, s2 * s2, 0.0) + exact_nt(
-        side_and_project, turned[:, : 2 * snap_count]
-    )
-    inverse[...] = eye.astype(f32)
-    size = 64
-    for start in range(0, modes, size):
-        stop = start + size
-        small = inverse_factor(lead[start:stop, start:stop], 8)
-        part = exact_nn(small, inverse[start:stop, :])
-        inverse[start:stop, :] = part
-        if stop < modes:
-            upper = exact_nn(small, lead[start:stop, :])
-            later = upper[:, stop:]
-            lead[stop:, :] -= exact_tn(later, upper)
-            inverse[stop:, :] -= exact_tn(later, part)
-
-    mine = inverse[pl.ds(pl.multiple_of(core * tile, tile), tile), :]
+    mine = own_inverse(project_t, s2, gram, first_core)
     both = exact_nn(mine, side_and_project)
     on_snaps = both[:, snap_count:]
     on_modes = mine * s2
@@ -417,27 +519,27 @@
         jnp.concatenate(
             [
                 jnp.where(first_core, on_first, on_second),
+                on_snaps,
                 jnp.where(first_core, on_second, on_first),
-                on_snaps,
             ],
             axis=1,
         )
     )
-    coef_hi[...], coef_lo[...] = coef
 
     def rotate(k, carry):
         for copy in loads(k):
             copy.wait()
         cols = piece(k)
-        result[:, cols] = dot3_nn((coef_hi[...], coef_lo[...]), split(rows[:, cols]))
+        value = dot3_nn(coef, (rows_hi[:, cols], rows_lo[:, cols]))
+        result[:, cols] = value * root[:, cols]
         pltpu.make_async_copy(result.at[:, cols], new_out.at[:, cols], out_sem.at[k]).start()
         return carry
 
     lax.fori_loop(0, chunks, rotate, 0)
 
     base = tile + mid + snap_count
-    swapped = (get(1, base + tile, tile), get(1, base, tile), get(1, base + modes, snap_count))
-    straight = (get(0, base, tile), get(0, base + tile, tile), get(0, base + modes, snap_count))
+    swapped = (get(1, base + tile, tile), get(1, base + modes, snap_count), get(1, base, tile))
+    straight = (get(0, base, tile), get(0, base + modes, snap_count), get(0, base + tile, tile))
     columns = jnp.concatenate(
         [
             jnp.concatenate(
@@ -456,45 +558,43 @@
     lax.fori_loop(0, chunks, finish, 0)
 
 
-def rotate(basis, other, snaps, total, singular):
-    tile, width = basis.shape
-    modes, snap_count = 2 * tile, snaps.shape[0]
+def rotate(cells, hi, lo, total, singular, volumes):
+    rows, width = hi.shape
+    modes = singular.shape[1]
+    tile = modes // 2
     chunks = width // CHUNK
     dma = pltpu.SemaphoreType.DMA
     vmem = pltpu.VMEM
     any_spec = pl.BlockSpec(memory_space=pl.ANY)
     vmem_spec = pl.BlockSpec(memory_space=vmem)
     return pl.pallas_call(
-        rotate_kernel,
+        functools.partial(rotate_kernel, cells),
         out_shape=(
             jax.ShapeDtypeStruct((tile, width), f32),
             jax.ShapeDtypeStruct((1, tile), f32),
             jax.ShapeDtypeStruct((tile, modes), f32),
         ),
-        in_specs=[any_spec] * 3 + [vmem_spec] * 2,
+        in_specs=[any_spec] * 2 + [vmem_spec] * 3,
         out_specs=(any_spec, vmem_spec, vmem_spec),
         scratch_shapes=[
-            vmem((modes + snap_count, width), f32),
+            vmem((rows, width), bf16),
+            vmem((rows, width), bf16),
             vmem((tile, width), f32),
-            vmem((modes, modes), f32),
-            vmem((modes, modes), f32),
-            vmem((tile, modes + snap_count), bf16),
-            vmem((tile, modes + snap_count), bf16),
-            dma((3, chunks)),
+            vmem((1, width), f32),
+            dma((2, chunks)),
             dma((chunks,)),
         ],
         compiler_params=pltpu.CompilerParams(vmem_limit_bytes=56 * 1024 * 1024),
-    )(basis, other, snaps, total, singular)
+    )(hi, lo, total, singular, volumes)
 
 
 def shards(basis, adjoint, snapshots, volumes, singular):
     tile, width = basis.shape
     cells = float(width * lax.axis_size("space"))
-    other, snaps, total = gather(
-        cells, basis, adjoint, snapshots, volumes.reshape(1, width)
-    )
+    volumes = volumes.reshape(1, width)
+    hi, lo, total = gather(cells, basis, adjoint, snapshots, volumes)
     new_tile, new_singular, hankel = rotate(
-        basis, other, snaps, total, singular.reshape(1, 2 * tile)
+        cells, hi, lo, total, singular.reshape(1, 2 * tile), volumes
     )
     return new_tile, new_singular.reshape(tile), hankel
 

time: 57.5 us -> 53.5 us (0.930)
  Pallas kernels: 56.7 us -> 52.7 us
    pallas_call x1, Pallas kernels: 19.6 us -> 15.4 us  [rotate(): pl.pallas_call(functools.partial(rotate_kernel, cells), out_shape=(jax.Sh...]
where the time goes in v5:
time: 53.5 us; the launch traced here: 53.3 us
  Pallas kernels  52.7 us (99%)
  between operations  0.64 us (1%)
    pallas_call x1, Pallas kernels, gather(): pl.pallas_call(functools.partial(gather_kernel, cells), out_shape=(jax.Sh...  37.3 us
    pallas_call x1, Pallas kernels, rotate(): pl.pallas_call(functools.partial(rotate_kernel, cells), out_shape=(jax.Sh...  15.4 us

profile of v5, /device:TPU:1, one launch (start us, length us, event | category | flops | bytes accessed | tf_op | source)
XLA Modules:
  0.0 53.3 jit_solution(5381906482490173654)
XLA Ops:
  0.6 37.3 %shard_map.76 = (bf16[288,8192]{1,0:T(8,128)(2,1)}, bf16[288,8192]{1,0:T(8,128)(2,1)}, f32[2,16,32,128]{3,2,1,0:T(8,128)}) custom-call(f32[128,8192]{1,0:T(8,128)} %basis.1, f32[128,8192]{1,0:T(8,128)} %adjoint.1, f32[16,8192]{1,0:T(8,128)} %snaps.1, f32[1,8192]{1,0:T(1,128)} %bitcast.3), custom_call_target="tpu_custom_call" | custom-call | tf_op jit(solution)/shard_map/pallas_call | solution.py:242
  37.9 15.4 %shard_map.77 = (f32[128,8192]{1,0:T(8,128)}, f32[1,128]{1,0:T(1,128)}, f32[128,256]{1,0:T(8,128)}) custom-call(bf16[288,8192]{1,0:T(8,128)(2,1)} %get-tuple-element.9.hi, bf16[288,8192]{1,0:T(8,128)(2,1)} %get-tuple-element.10.lo, f32[2,16,32,128]{3,2,1,0:T(8,128)} %get-tuple-element.11.total, f32[1,256]{1,0:T(1,128)} %bitcast.5, f32[1,8192]{1,0:T(1,128)} %bitcast.4), custom_call_target="tpu_custom_call" | custom-call | tf_op jit(solution)/shard_map/pallas_call | solution.py:570

commit v6 on v5

--- a/solution.py
+++ b/solution.py
@@ -14,6 +14,7 @@
 SIDE = 4
 PLANE = SIDE * SIDE
 CHUNK = 1024
+TURN = 2048
 
 
 def split(value):
@@ -44,10 +45,10 @@
 def gather_kernel(
     cells,
     basis, adjoint, snaps, volumes,
-    hi_out, lo_out, total_out,
+    hi_out, lo_out, total,
     own, other, adj, snap, root,
-    left_hi, left_lo, adj_hi, adj_lo,
-    acc, acc_snap, share, slots, part, z_slots, total,
+    left_hi, left_lo, right_hi, right_lo,
+    acc, acc_snap, share, slots, part, z_slots,
     load_sem, adj_sem, small_sem, bs_sem, br_sem, ss_sem, out_sem,
     rs_sem, rr_sem, zs_sem, zr_sem, gs_sem, gr_sem, fs_sem, fr_sem,
 ):
@@ -115,9 +116,11 @@
     def prepare(k, carry):
         cols = piece(k)
         load_own(k).wait()
-        left_hi[:tile, cols], left_lo[:tile, cols] = split(own[:, cols] * root[:, cols])
+        high, low = split(own[:, cols] * root[:, cols])
+        left_hi[:tile, cols], left_lo[:tile, cols] = high, low
+        right_hi[:tile, cols], right_lo[:tile, cols] = high, low
         load_adj(k).wait()
-        adj_hi[:, cols], adj_lo[:, cols] = split(adj[:, cols] * root[:, cols])
+        right_hi[tile:, cols], right_lo[tile:, cols] = split(adj[:, cols] * root[:, cols])
         return carry
 
     lax.fori_loop(0, chunks, prepare, 0)
@@ -138,10 +141,7 @@
         left_hi[near:, cols], left_lo[near:, cols] = split(other[:, cols] * root[:, cols])
         for copy in saves(k):
             copy.start()
-        right = tuple(
-            jnp.concatenate([a[:tile, cols], b[:, cols]], axis=0)
-            for a, b in ((left_hi, adj_hi), (left_lo, adj_lo))
-        )
+        right = (right_hi[:, cols], right_lo[:, cols])
         acc[...] += dot3((left_hi[:, cols], left_lo[:, cols]), right)
         both = (left_hi[tile:near, cols], left_lo[tile:near, cols])
         acc_snap[...] += dot3(both, both)
@@ -216,7 +216,6 @@
         f_copies[-1].start()
     for copy in f_copies:
         copy.wait()
-    total_out[...] = total[...]
     for copy in copies + z_copies + g_copies:
         copy.wait_send()
 
@@ -256,15 +255,14 @@
             vmem((1, width), f32),
             vmem((rows, width), bf16),
             vmem((rows, width), bf16),
-            vmem((tile, width), bf16),
-            vmem((tile, width), bf16),
+            vmem((2 * tile, width), bf16),
+            vmem((2 * tile, width), bf16),
             vmem((rows, 2 * tile), f32),
             vmem((snap_count, snap_count), f32),
             vmem((PLANE, flat, tile), f32),
             vmem((PLANE, flat, tile), f32),
             vmem((2, flat, tile), f32),
             vmem((SIDE, flat, tile), f32),
-            vmem((2, PLANE, flat, tile), f32),
             dma((chunks,)),
             dma((chunks,)),
             dma((1,)),
@@ -448,12 +446,12 @@
     modes = 2 * tile
     snap_count = hi.shape[0] - modes
     near = tile + snap_count
-    chunks = width // CHUNK
+    chunks = width // TURN
     core = lax.axis_index("mode")
     first_core = core == 0
 
     def piece(k):
-        return pl.ds(pl.multiple_of(k * CHUNK, CHUNK), CHUNK)
+        return pl.ds(pl.multiple_of(k * TURN, TURN), TURN)
 
     def loads(k):
         cols = piece(k)
@@ -562,7 +560,7 @@
     rows, width = hi.shape
     modes = singular.shape[1]
     tile = modes // 2
-    chunks = width // CHUNK
+    chunks = width // TURN
     dma = pltpu.SemaphoreType.DMA
     vmem = pltpu.VMEM
     any_spec = pl.BlockSpec(memory_space=pl.ANY)

time: 53.5 us -> 53 us (level)
  Pallas kernels: 52.7 us -> 52.1 us
where the time goes in v6:
time: 53 us; the launch traced here: 52.8 us
  Pallas kernels  52.1 us (98%)
  between operations  0.64 us (1%)
    pallas_call x1, Pallas kernels, gather(): pl.pallas_call(functools.partial(gather_kernel, cells), out_shape=(jax.Sh...  37.2 us
    pallas_call x1, Pallas kernels, rotate(): pl.pallas_call(functools.partial(rotate_kernel, cells), out_shape=(jax.Sh...  15 us

profile of v6, /device:TPU:1, one launch (start us, length us, event | category | flops | bytes accessed | tf_op | source)
XLA Modules:
  0.0 52.8 jit_solution(17231906885317744415)
XLA Ops:
  0.6 37.2 %shard_map.76 = (bf16[288,8192]{1,0:T(8,128)(2,1)}, bf16[288,8192]{1,0:T(8,128)(2,1)}, f32[2,16,32,128]{3,2,1,0:T(8,128)}) custom-call(f32[128,8192]{1,0:T(8,128)} %basis.1, f32[128,8192]{1,0:T(8,128)} %adjoint.1, f32[16,8192]{1,0:T(8,128)} %snaps.1, f32[1,8192]{1,0:T(1,128)} %bitcast.3), custom_call_target="tpu_custom_call" | custom-call | tf_op jit(solution)/shard_map/pallas_call | solution.py:241
  37.8 15.0 %shard_map.77 = (f32[128,8192]{1,0:T(8,128)}, f32[1,128]{1,0:T(1,128)}, f32[128,256]{1,0:T(8,128)}) custom-call(bf16[288,8192]{1,0:T(8,128)(2,1)} %get-tuple-element.9.hi, bf16[288,8192]{1,0:T(8,128)(2,1)} %get-tuple-element.10.lo, f32[2,16,32,128]{3,2,1,0:T(8,128)} %get-tuple-element.11.total, f32[1,256]{1,0:T(1,128)} %bitcast.5, f32[1,8192]{1,0:T(1,128)} %bitcast.4), custom_call_target="tpu_custom_call" | custom-call | tf_op jit(solution)/shard_map/pallas_call | solution.py:568

commit v7 on v6

--- a/solution.py
+++ b/solution.py
@@ -73,7 +73,8 @@
         return (lax.rem(level + step, SIDE) * PLANE + spot, core)
 
     def piece(k):
-        return pl.ds(pl.multiple_of(k * CHUNK, CHUNK), CHUNK)
+        start = k * CHUNK
+        return pl.ds(start if isinstance(k, int) else pl.multiple_of(start, CHUNK), CHUNK)
 
     def load_own(k):
         return pltpu.make_async_copy(basis.at[:, piece(k)], own.at[:, piece(k)], load_sem.at[k])
@@ -147,7 +148,18 @@
         acc_snap[...] += dot3(both, both)
         return carry
 
-    lax.fori_loop(0, chunks, multiply, 0)
+    lax.fori_loop(0, chunks - 1, multiply, 0)
+
+    cols = piece(chunks - 1)
+    right = (right_hi[:, cols], right_lo[:, cols])
+    acc[:near] += dot3((left_hi[:near, cols], left_lo[:near, cols]), right)
+    both = (left_hi[tile:near, cols], left_lo[tile:near, cols])
+    acc_snap[...] += dot3(both, both)
+    send_own(chunks - 1).wait_recv()
+    left_hi[near:, cols], left_lo[near:, cols] = split(other[:, cols] * root[:, cols])
+    for copy in saves(chunks - 1):
+        copy.start()
+    acc[near:] += dot3((left_hi[near:, cols], left_lo[near:, cols]), right)
 
     mid = tile // 2
     flat = share.shape[1]

time: 53 us -> 54.1 us (1.021)
  Pallas kernels: 52.1 us -> 53.2 us
    pallas_call x1, Pallas kernels: 37.2 us -> 38.3 us  [gather(): pl.pallas_call(functools.partial(gather_kernel, cells), out_shape=(jax.Sh...]
where the time goes in v7:
time: 54.1 us; the launch traced here: 53.9 us
  Pallas kernels  53.2 us (98%)
  between operations  0.64 us (1%)
    pallas_call x1, Pallas kernels, gather(): pl.pallas_call(functools.partial(gather_kernel, cells), out_shape=(jax.Sh...  38.3 us
    pallas_call x1, Pallas kernels, rotate(): pl.pallas_call(functools.partial(rotate_kernel, cells), out_shape=(jax.Sh...  15 us

profile of v7, /device:TPU:1, one launch (start us, length us, event | category | flops | bytes accessed | tf_op | source)
XLA Modules:
  0.0 53.9 jit_solution(9117875283947281753)
XLA Ops:
  0.6 38.3 %shard_map.76 = (bf16[288,8192]{1,0:T(8,128)(2,1)}, bf16[288,8192]{1,0:T(8,128)(2,1)}, f32[2,16,32,128]{3,2,1,0:T(8,128)}) custom-call(f32[128,8192]{1,0:T(8,128)} %basis.1, f32[128,8192]{1,0:T(8,128)} %adjoint.1, f32[16,8192]{1,0:T(8,128)} %snaps.1, f32[1,8192]{1,0:T(1,128)} %bitcast.3), custom_call_target="tpu_custom_call" | custom-call | tf_op jit(solution)/shard_map/pallas_call | solution.py:253
  38.9 15.0 %shard_map.77 = (f32[128,8192]{1,0:T(8,128)}, f32[1,128]{1,0:T(1,128)}, f32[128,256]{1,0:T(8,128)}) custom-call(bf16[288,8192]{1,0:T(8,128)(2,1)} %get-tuple-element.9.hi, bf16[288,8192]{1,0:T(8,128)(2,1)} %get-tuple-element.10.lo, f32[2,16,32,128]{3,2,1,0:T(8,128)} %get-tuple-element.11.total, f32[1,256]{1,0:T(1,128)} %bitcast.5, f32[1,8192]{1,0:T(1,128)} %bitcast.4), custom_call_target="tpu_custom_call" | custom-call | tf_op jit(solution)/shard_map/pallas_call | solution.py:580
